TPU v7x, 128 devices: a whole 4x4x4 slice. The times are simulated.
128 devices in a mesh: row: 16 (over x, y), col: 8 (over z, core).
Axes of the slice: x: 4, y: 4, z: 4, core: 2. Of those that a mesh axis runs over, the one named last changes fastest.
Arguments:
- nodes: bfloat16 [49152, 768], P(('row', 'col')), may hold values from -6 to 6
- w_query: bfloat16 [768, 768], replicated, may hold values from -0.4375 to 0.4375
- w_key: bfloat16 [768, 768], replicated, may hold values from -0.21875 to 0.21875
- w_value: bfloat16 [768, 768], replicated, may hold values from -0.21875 to 0.21875
- w_out: bfloat16 [768, 768], replicated, may hold values from -0.21875 to 0.21875
- w_edge_gate: bfloat16 [64, 8], replicated, may hold values from -0.75 to 0.75
- w_edge_bias: bfloat16 [64, 8], replicated, may hold values from -0.75 to 0.75
- w_edge_out: float32 [8, 64], replicated, may hold values from -2 to 2
- gain_node: float32 [768], replicated, may hold values from 0.1 to 1.9
- gain_edge: float32 [64], replicated, may hold values from 0.1 to 1.9
- edges: bfloat16 [16, 8, 4, 64, 128, 128], P('row', 'col'), may hold values from -6 to 6
- tile_list: int32 [16, 8, 4], P('row', 'col'), may hold values from 0 to 1151, as said below
- tile_count: int32 [16, 8], P('row', 'col'), may hold values from 1 to 4, as said below
Outputs:
- nodes_out: bfloat16 [49152, 768], P(('row', 'col'))
- edges_out: bfloat16 [16, 8, 4, 64, 128, 128], P('row', 'col')
Inputs may be any that keep to these rules, and one draw needn't show every extreme that they name: `tile_list`: the destination blocks of the 4 slots of one device are distinct. `tile_count`: some device has all 4 slots live.
All inputs are finite; a program needn't handle non-finite values.
Results may differ from a plain program's by a relative error of at most 0.0075.
Values may be sent and summed in bfloat16 or wider, within the bound.
A program may use at most 192 MiB of HBM per device.

v0:
```python
import jax
import jax.numpy as jnp
from jax import lax
from jax.sharding import PartitionSpec as P

HEADS = 8
BLOCK = 128


def tile_step(query_block, pair_block, edge, w_edge_mix, w_edge_out, gain_edge, is_live):
    width = query_block.shape[1]
    head_dim = width // HEADS
    query_heads = query_block.reshape(BLOCK, HEADS, head_dim)
    key_heads = pair_block[:, :width].reshape(BLOCK, HEADS, head_dim)
    value_heads = pair_block[:, width:].reshape(BLOCK, HEADS, head_dim)
    raw = jnp.einsum("ihd,jhd->hij", query_heads, key_heads, preferred_element_type=jnp.float32) * (
        1.0 / head_dim**0.5
    )
    edge_terms = jnp.einsum("cij,ck->kij", edge, w_edge_mix, preferred_element_type=jnp.float32)
    bias = edge_terms[:HEADS]
    gate = edge_terms[HEADS:]
    score = jnp.clip(raw, -5.0, 5.0) + bias
    expo = jnp.exp(score) * is_live
    weight = expo * jax.nn.sigmoid(gate)
    denom_part = jnp.sum(expo, axis=2).T
    numer_part = jnp.einsum(
        "hij,jhd->ihd", weight.astype(jnp.bfloat16), value_heads, preferred_element_type=jnp.float32
    ).reshape(BLOCK, width)
    edge_mixed = edge.astype(jnp.float32) + jnp.einsum(
        "hij,hc->cij", score, w_edge_out, precision=lax.Precision.HIGHEST
    )
    square_mean = jnp.mean(edge_mixed * edge_mixed, axis=0, keepdims=True)
    edge_new = edge_mixed * lax.rsqrt(square_mean + 1e-05) * gain_edge[:, None, None] * is_live
    return (numer_part, denom_part, edge_new.astype(jnp.bfloat16))


def on_device(
    nodes,
    w_query,
    w_key,
    w_value,
    w_out,
    w_edge_gate,
    w_edge_bias,
    w_edge_out,
    gain_node,
    gain_edge,
    edges,
    tile_list,
    tile_count,
):
    own_rows = nodes.shape[0]
    width = nodes.shape[1]
    head_dim = width // HEADS
    query_own = jnp.dot(nodes, w_query, preferred_element_type=jnp.float32).astype(jnp.bfloat16)
    queries = lax.all_gather(query_own, "col", axis=0, tiled=True)
    w_pair = jnp.concatenate([w_key, w_value], axis=1)
    pair_own = jnp.dot(nodes, w_pair, preferred_element_type=jnp.float32).astype(jnp.bfloat16)
    sources = lax.all_gather(pair_own, "row", axis=0, tiled=True)
    w_edge_mix = jnp.concatenate([w_edge_bias, w_edge_gate], axis=1)
    src_blocks = sources.shape[0] // BLOCK
    dest_rows = queries.shape[0]
    numer = jnp.zeros((dest_rows, width), jnp.float32)
    denom = jnp.zeros((dest_rows, HEADS), jnp.float32)
    live_count = tile_count[0, 0]
    new_edges = []
    for slot in range(edges.shape[2]):
        tile = tile_list[0, 0, slot]
        dest_start = tile // src_blocks * BLOCK
        src_start = tile % src_blocks * BLOCK
        is_live = (slot < live_count).astype(jnp.float32)
        query_block = lax.dynamic_slice_in_dim(queries, dest_start, BLOCK, 0)
        pair_block = lax.dynamic_slice_in_dim(sources, src_start, BLOCK, 0)
        numer_part, denom_part, edge_new = tile_step(
            query_block, pair_block, edges[0, 0, slot], w_edge_mix, w_edge_out, gain_edge, is_live
        )
        numer = lax.dynamic_update_slice_in_dim(
            numer, lax.dynamic_slice_in_dim(numer, dest_start, BLOCK, 0) + numer_part, dest_start, 0
        )
        denom = lax.dynamic_update_slice_in_dim(
            denom, lax.dynamic_slice_in_dim(denom, dest_start, BLOCK, 0) + denom_part, dest_start, 0
        )
        new_edges.append(edge_new)
    edges_out = jnp.stack(new_edges, axis=0)[None, None]
    numer_all, denom_all = (
        lax.psum(numer.astype(jnp.bfloat16), "col").astype(jnp.float32),
        lax.psum(denom.astype(jnp.bfloat16), "col").astype(jnp.float32),
    )
    own_start = lax.axis_index("col") * own_rows
    numer = lax.dynamic_slice_in_dim(numer_all, own_start, own_rows, 0)
    denom = lax.dynamic_slice_in_dim(denom_all, own_start, own_rows, 0)
    safe_denom = jnp.where(denom > 0.0, denom, 1.0)
    attended = (
        (numer.reshape(own_rows, HEADS, head_dim) / safe_denom[:, :, None])
        .reshape(own_rows, width)
        .astype(jnp.bfloat16)
    )
    mixed = nodes.astype(jnp.float32) + jnp.dot(attended, w_out, preferred_element_type=jnp.float32)
    square_mean = jnp.mean(mixed * mixed, axis=1, keepdims=True)
    nodes_out = (mixed * lax.rsqrt(square_mean + 1e-05) * gain_node).astype(jnp.bfloat16)
    return (nodes_out, edges_out)


def solution(mesh):
    return jax.shard_map(
        on_device,
        mesh=mesh,
        in_specs=(
            P(("row", "col"), None),
            P(),
            P(),
            P(),
            P(),
            P(),
            P(),
            P(),
            P(),
            P(),
            P("row", "col", None, None, None, None),
            P("row", "col", None),
            P("row", "col"),
        ),
        out_specs=(P(("row", "col"), None), P("row", "col", None, None, None, None)),
        check_vma=False,
    )
```

profile of v0, /device:TPU:1, one launch (start us, length us, event | category | flops | bytes accessed | tf_op | source)
XLA Modules:
  0.0 316.8 jit_solution(13145858343724698212)
XLA Ops:
  7.2 3.0 convolution_convert_fusion.1
  10.3 4.2 %fusion = bf16[384,1536]{0,1:T(8,128)(2,1)} fusion(bf16[384,768]{1,0:T(8,128)(2,1)} %param.13, bf16[768,768]{1,0:T(8,128)(2,1)} %param.16, bf16[768,768]{1,0:T(8,128)(2,1)} %param.15), kind=kOutput, calls=%fused_computation.14 | convolution fusion | flops 911278080 | bytes 4128768 | tf_op jit(solution)/shard_map/dot_general | solution.py:58
  23.3 6.2 %fusion.45 = (bf16[1,1,1,64,128,128]{5,4,3,2,1,0:T(8,128)(2,1)S(1)}, bf16[1,1,1,64,128,128]{5,4,3,2,1,0:T(8,128)(2,1)}, bf16[1,1,1,64,128,128]{5,4,3,2,1,0:T(8,128)(2,1)}, bf16[1,1,1,64,128,128]{5,4,3,2,1,0:T(8,128)(2,1)S(1)}) fusion(bf16[1,1,4,64,128,128]{5,4,3,2,1,0:T(8,128)(2,1)} %param.23), kind=kLoop, calls=%fused_computation.109 | loop fusion | bytes 16777216 | tf_op jit(solution)/shard_map/slice | solution.py:75
  29.5 1.4 copy-done.3
  30.9 1.2 fusion.8
  32.1 1.1 fusion.49
  33.2 2.1 copy.67
  35.9 2.1 copy.66
  38.0 2.8 fusion.9
  40.8 1.1 fusion.48
  41.9 2.1 copy.70
  44.0 2.0 copy.69
  46.0 2.8 fusion.10
  48.9 1.0 fusion.47
  49.9 2.0 copy.73
  51.9 2.1 copy.72
  54.0 1.2 fusion.11
  55.2 1.1 fusion.46
  56.3 2.0 copy.76
  58.3 2.1 copy.75
  60.4 2.2 constant_dynamic-slice_fusion.3
  62.6 1.7 copy.36
  64.3 1.8 copy.41
  66.1 1.8 copy.46
  67.8 0.8 copy.51
  68.6 112.2 %all-gather.3.cloned.1.call-done = bf16[6144,1536]{0,1:T(8,128)(2,1)} async-done(((bf16[384,1536]{0,1:T(8,128)(2,1)}), bf16[6144,1536]{0,1:T(8,128)(2,1)}) %all-gather.3.cloned.1.call-update) | async-done | bytes 18874384 | tf_op jit(solution)/shard_map/all_gather | solution.py:59
  180.8 2.6 constant_dynamic-slice_fusion.4
  183.4 2.3 fusion.21
  185.7 2.0 copy.56
  187.7 2.4 fusion.22
  190.1 2.0 copy.57
  192.1 2.4 fusion.24
  194.5 2.0 copy.59
  196.5 2.3 fusion.23
  198.8 2.1 copy.58
  200.9 1.6 fusion.25
  202.6 1.2 broadcast_in_dim.9
  206.0 3.0 convert_element_type.106
  209.7 6.6 %multiply_reduce_fusion.3 = (f32[128,128]{1,0:T(8,128)S(1)}, f32[128,128,64]{1,2,0:T(8,128)S(1)}) fusion(bf16[1,1,1,64,128,128]{5,4,3,2,1,0:T(8,128)(2,1)} %copy-done.3, f32[8,128,128]{2,0,1:T(8,128)} %copy.56, f32[8,64]{1,0:T(8,128)S(1)} %copy-done.17), kind=kOutput, calls=%fused_computation.12 | convolution fusion | flops 104841216 | bytes 6883328 | tf_op jit(solution)/shard_map/hij,hc->cij/dot_general | solution.py:29
  216.3 4.7 %multiply_reduce_fusion.2 = (f32[128,128]{1,0:T(8,128)S(1)}, f32[128,128,64]{1,2,0:T(8,128)S(1)}) fusion(bf16[1,1,1,64,128,128]{5,4,3,2,1,0:T(8,128)(2,1)S(1)} %copy-done.2, f32[8,128,128]{2,0,1:T(8,128)S(1)} %copy-done.5, f32[8,64]{1,0:T(8,128)S(1)} %copy-done.17), kind=kOutput, calls=%fused_computation.10 | convolution fusion | flops 104841216 | bytes 6883328 | tf_op jit(solution)/shard_map/hij,hc->cij/dot_general | solution.py:29
  221.0 9.6 %multiply_reduce_fusion = (f32[128,128]{1,0:T(8,128)S(1)}, f32[128,128,64]{1,2,0:T(8,128)}) fusion(bf16[1,1,1,64,128,128]{5,4,3,2,1,0:T(8,128)(2,1)S(1)} %get-tuple-element.14, f32[8,128,128]{2,0,1:T(8,128)S(1)} %copy-done.6, f32[8,64]{1,0:T(8,128)S(1)} %copy-done.17), kind=kOutput, calls=%fused_computation.6 | convolution fusion | flops 104841216 | bytes 6883328 | tf_op jit(solution)/shard_map/hij,hc->cij/dot_general | solution.py:29
  230.6 9.4 %multiply_reduce_fusion.1 = (f32[128,128]{1,0:T(8,128)S(1)}, f32[128,128,64]{1,2,0:T(8,128)}) fusion(bf16[1,1,1,64,128,128]{5,4,3,2,1,0:T(8,128)(2,1)S(1)} %copy-done.1, f32[8,128,128]{2,0,1:T(8,128)S(1)} %copy-done.7, f32[8,64]{1,0:T(8,128)S(1)} %copy-done.17), kind=kOutput, calls=%fused_computation.8 | convolution fusion | flops 104841216 | bytes 6883328 | tf_op jit(solution)/shard_map/hij,hc->cij/dot_general | solution.py:29
  240.0 23.5 %fusion.4 = (bf16[1,64,128,128]{3,1,2,0:T(8,128)(2,1)}, bf16[1,64,128,128]{3,1,2,0:T(8,128)(2,1)}, bf16[1,64,128,128]{3,1,2,0:T(8,128)(2,1)}, bf16[1,64,128,128]{3,1,2,0:T(8,128)(2,1)}) fusion(f32[128,128,64]{1,2,0:T(8,128)S(1)} %get-tuple-element.49, f32[]{:T(128)} %bitcast.9, f32[64]{0:T(128)S(1)} %copy-done.22, f32[128,128]{1,0:T(8,128)S(1)} %get-tuple-element.59, ...), kind=kLoop, calls=%fused_computation.18 | loop fusion | flops 25165824 | bytes 33816848 | tf_op jit(solution)/shard_map/stack | solution.py:84
  263.5 7.5 %maximum_bitcast_fusion = bf16[1,1,4,64,128,128]{5,3,4,2,1,0:T(8,128)(2,1)} fusion(bf16[1,64,128,128]{3,1,2,0:T(8,128)(2,1)} %get-tuple-element.33, bf16[1,64,128,128]{3,1,2,0:T(8,128)(2,1)} %get-tuple-element.32, bf16[1,64,128,128]{3,1,2,0:T(8,128)(2,1)} %get-tuple-element.31, bf16[1,64,128,128]{3,1,2,0:T(8,128)(2,1)} %get-tuple-element.30), kind=kLoop, calls=%fused_computation | loop fusion | flops 12582912 | bytes 16777216 | tf_op jit(solution)/shard_map/broadcast_in_dim | solution.py:84
  271.1 12.4 %copy.60 = bf16[1,1,4,64,128,128]{5,4,3,2,1,0:T(8,128)(2,1)} copy(bf16[1,1,4,64,128,128]{5,3,4,2,1,0:T(8,128)(2,1)} %maximum_bitcast_fusion) | data formatting | bytes 16777216
  283.5 23.5 %psum.15 = bf16[3072,8]{0,1:T(8,128)(2,1)S(1)} all-reduce(bf16[3072,8]{0,1:T(8,128)(2,1)S(1)} %convert_element_type.108), channel_id=1, replica_groups=mesh['row'=16,'col'=8] {'col'}, use_global_device_ids=true, to_apply=%region_5.6 | all-reduce | flops 24576 | bytes 98304 | tf_op jit(solution)/shard_map/psum | solution.py:87
  307.0 1.2 fusion.20
  309.0 1.0 multiply_convert_fusion.4
  (74 shorter events, 4.5 us)
Async XLA Ops:
  7.2 301.0 %copy-start = (bf16[768,768]{1,0:T(8,128)(2,1)S(1)}, bf16[768,768]{1,0:T(8,128)(2,1)}, u32[]{:S(2)}) copy-start(bf16[768,768]{1,0:T(8,128)(2,1)} %param.17) | copy-start | bytes 3538948
  7.2 53.2 %all-gather.5.cloned.1.call-start = ((), (), s32[]{:S(2)}) async-start(), calls=%async_computation.1 | async-start | bytes 5308416 | tf_op jit(solution)/shard_map/all_gather | solution.py:56
  10.2 4.4 %copy-start.20 = (s32[1,1,4]{2,1,0:T(1,128)S(1)}, s32[1,1,4]{2,1,0:T(1,128)}, u32[]{:S(2)}) copy-start(s32[1,1,4]{2,1,0:T(1,128)} %param.24) | copy-start | bytes 52
  10.2 170.6 %all-gather.3.cloned.1.call-start = ((), (), s32[]{:S(2)}) async-start(), calls=%async_computation | async-start | bytes 20054016 | tf_op jit(solution)/shard_map/all_gather | solution.py:59
  14.5 292.4 %all-reduce.2.cloned.1.call-start = ((), (), s32[]{:S(2)}) async-start(), calls=%async_computation.2 | async-start | bytes 9437184 | tf_op jit(solution)/shard_map/psum | solution.py:86
  23.3 7.6 %copy-start.18 = (bf16[64,8]{0,1:T(8,128)(2,1)S(1)}, bf16[64,8]{0,1:T(8,128)(2,1)}, u32[]{:S(2)}) copy-start(bf16[64,8]{0,1:T(8,128)(2,1)} %param.18) | copy-start | bytes 3076
  23.3 7.6 %copy-start.19 = (bf16[64,8]{0,1:T(8,128)(2,1)S(1)}, bf16[64,8]{0,1:T(8,128)(2,1)}, u32[]{:S(2)}) copy-start(bf16[64,8]{0,1:T(8,128)(2,1)} %param.19) | copy-start | bytes 3076
  29.5 1.4 copy-start.3
  202.5 1.3 copy-start.9
  202.5 1.3 copy-start.11
  202.5 1.3 copy-start.16
  203.7 1.1 copy-start.10
  203.7 1.2 copy-start.12
  203.7 1.2 copy-start.15
  203.7 1.7 copy-start.8
  203.8 1.7 copy-start.13
  203.8 1.7 copy-start.14
  209.0 0.7 copy-start.17
  209.0 7.2 %copy-start.2 = (bf16[1,1,1,64,128,128]{5,4,3,2,1,0:T(8,128)(2,1)S(1)}, bf16[1,1,1,64,128,128]{5,4,3,2,1,0:T(8,128)(2,1)}, u32[]{:S(2)}) copy-start(bf16[1,1,1,64,128,128]{5,4,3,2,1,0:T(8,128)(2,1)} %get-tuple-element.16) | copy-start | bytes 6291460
  209.0 7.2 %copy-start.5 = (f32[8,128,128]{2,0,1:T(8,128)S(1)}, f32[8,128,128]{2,0,1:T(8,128)}, u32[]{:S(2)}) copy-start(f32[8,128,128]{2,0,1:T(8,128)} %copy.57) | copy-start | bytes 1572868
  216.3 4.7 %copy-start.6 = (f32[8,128,128]{2,0,1:T(8,128)S(1)}, f32[8,128,128]{2,0,1:T(8,128)}, u32[]{:S(2)}) copy-start(f32[8,128,128]{2,0,1:T(8,128)} %copy.59) | copy-start | bytes 1572868
  221.0 9.6 %copy-start.1 = (bf16[1,1,1,64,128,128]{5,4,3,2,1,0:T(8,128)(2,1)S(1)}, bf16[1,1,1,64,128,128]{5,4,3,2,1,0:T(8,128)(2,1)}, u32[]{:S(2)}) copy-start(bf16[1,1,1,64,128,128]{5,4,3,2,1,0:T(8,128)(2,1)} %get-tuple-element.15) | copy-start | bytes 6291460
  221.0 9.6 %copy-start.7 = (f32[8,128,128]{2,0,1:T(8,128)S(1)}, f32[8,128,128]{2,0,1:T(8,128)}, u32[]{:S(2)}) copy-start(f32[8,128,128]{2,0,1:T(8,128)} %copy.58) | copy-start | bytes 1572868
  230.6 9.4 %copy-start.4 = (bf16[1,1,1,64,128,128]{5,4,3,2,1,0:T(8,128)(2,1)S(1)}, bf16[1,1,1,64,128,128]{5,4,3,2,1,0:T(8,128)(2,1)}, u32[]{:S(2)}) copy-start(bf16[1,1,1,64,128,128]{5,4,3,2,1,0:T(8,128)(2,1)} %copy-done.3) | copy-start | bytes 6291460
  230.6 9.4 %copy-start.22 = (f32[64]{0:T(128)S(1)}, f32[64]{0:T(128)}, u32[]{:S(2)}) copy-start(f32[64]{0:T(128)} %param.22) | copy-start | bytes 772
  271.1 37.1 %copy-start.23 = (bf16[384,768]{1,0:T(8,128)(2,1)S(1)}, bf16[384,768]{1,0:T(8,128)(2,1)}, u32[]{:S(2)}) copy-start(bf16[384,768]{1,0:T(8,128)(2,1)} %param.13) | copy-start | bytes 1769476
  283.5 25.5 %copy-start.21 = (f32[768]{0:T(1024)S(1)}, f32[768]{0:T(1024)}, u32[]{:S(2)}) copy-start(f32[768]{0:T(1024)} %param.21) | copy-start | bytes 9220
Sparse Core Ops, SparseCore 0:
  10.4 38.1 all-gather.4
  50.7 130.1 all-gather.2
  209.1 73.3 all-reduce.1
where the time goes:
time: 323 us; the launch traced here: 317 us
  waiting for transfers between devices  112 us (35%)
  local copies, waits for them, and re-layouts  62.8 us (19%)
  matrix products  58.3 us (18%)
  other arithmetic  36.7 us (11%)
  blocking collectives  23.5 us (7%)
  between operations  23.2 us (7%)
    all_gather x1, waiting for transfers between devices, on_device(): sources = lax.all_gather(pair_own, 'row', axis=0, tiled=True)  112 us
    unnamed x57, local copies, waits for them, and re-layouts  31.5 us
    dot_general x4, matrix products, tile_step(): jnp.einsum('hij,hc->cij', score, w_edge_out, precision=lax.Precision.HIGH...  30.2 us
    another operation x1, other arithmetic, on_device(): edges_out = jnp.stack(new_edges, axis=0)[None, None]  23.5 us
    psum x1, blocking collectives, on_device(): lax.psum(denom.astype(jnp.bfloat16), 'col').astype(jnp.float32)  23.5 us
    dot_general x4, matrix products, tile_step(): jnp.einsum('ihd,jhd->hij', query_heads, key_heads, preferred_element_type...  9.33 us
    dynamic_slice x5, local copies, waits for them, and re-layouts, on_device(): query_block = lax.dynamic_slice_in_dim(queries, dest_start, BLOCK, 0)  8.23 us
    add x4, local copies, waits for them, and re-layouts, tile_step(): score = jnp.clip(raw, -5.0, 5.0) + bias  8.17 us
  transfers between devices with their start and end apart: 3, of which 1 were waited for; matrix products, arithmetic and copies ran while one was open for 38% of the time, Pallas kernels for 0%

commit v1 on v0

v1 whole, which is shorter than its diff:
```python
import jax
import jax.numpy as jnp
from jax import lax
from jax.experimental import pallas as pl
from jax.experimental.pallas import tpu as pltpu
from jax.sharding import PartitionSpec as P

HEADS = 8
BLOCK = 128
CH = 64
GROUP = 16
F32 = jnp.float32
BF16 = jnp.bfloat16
NT = (((1,), (1,)), ((), ()))


def iota(shape, dim):
    return lax.broadcasted_iota(jnp.int32, shape, dim)


def dot(a, b, dims=(((1,), (0,)), ((), ()))):
    return lax.dot_general(a, b, dims, preferred_element_type=F32)


def where01(mask):
    return jnp.where(mask, 1.0, 0.0).astype(BF16)


def build_maps(wb_ref, wg_ref, wo_ref, mix_map, out_map):
    rows, cols = 2 * HEADS * GROUP, CH * GROUP
    pick = iota((rows, HEADS), 0) // GROUP
    head = iota((rows, HEADS), 1)
    picked = dot(where01(pick == head), wb_ref[...], NT) + dot(
        where01(pick == head + HEADS), wg_ref[...], NT
    )
    spread = where01(iota((CH, cols), 0) == iota((CH, cols), 1) // GROUP)
    full = dot(picked.astype(BF16), spread)
    same = iota((rows, cols), 0) % GROUP == iota((rows, cols), 1) % GROUP
    mix_map[...] = jnp.where(same, full, 0.0).astype(BF16)
    narrow = HEADS * GROUP
    w_out = wo_ref[...]
    high = w_out.astype(BF16)
    low = (w_out - high.astype(F32)).astype(BF16)
    pick = where01(iota((cols, CH), 0) // GROUP == iota((cols, CH), 1))
    spread = where01(iota((HEADS, narrow), 0) == iota((HEADS, narrow), 1) // GROUP)
    same = iota((cols, narrow), 0) % GROUP == iota((cols, narrow), 1) % GROUP
    for part, w in enumerate((high, low)):
        full = dot(dot(pick, w, NT).astype(BF16), spread)
        out_map[:, part * narrow : (part + 1) * narrow] = jnp.where(same, full, 0.0).astype(BF16)


def tile_kernel(
    count_ref,
    gain_ref,
    dest_ref,
    src_ref,
    wq_ref,
    wk_ref,
    wv_ref,
    wb_ref,
    wg_ref,
    wo_ref,
    edge_ref,
    numer_ref,
    denom_ref,
    out_ref,
    q_s,
    k_s,
    v_s,
    mix_map,
    out_map,
    raw_s,
    weight_s,
    expo_s,
    mixed_s,
):
    slot = pl.program_id(0)
    width = q_s.shape[-1]
    head_dim = width // HEADS
    tiles = width // 128

    @pl.when(slot == 0)
    def _():
        build_maps(wb_ref, wg_ref, wo_ref, mix_map, out_map)
        for w_ref, x_ref, y_s in ((wq_ref, dest_ref, q_s), (wk_ref, src_ref, k_s), (wv_ref, src_ref, v_s)):
            x = x_ref[...].reshape(-1, width)
            for n in range(0, width, 256):
                y = dot(x, w_ref[:, n : n + 256]).astype(BF16)
                y_s[:, :, n : n + 256] = y.reshape(-1, BLOCK, 256)

    @pl.when(slot >= count_ref[0])
    def _():
        numer_ref[...] = jnp.zeros_like(numer_ref)
        denom_ref[...] = jnp.zeros_like(denom_ref)
        out_ref[...] = jnp.zeros_like(out_ref)

    @pl.when(slot < count_ref[0])
    def _():
        for h in range(HEADS):
            lo, hi = h * head_dim, (h + 1) * head_dim
            a, b = lo // 128 * 128, -(-hi // 128) * 128
            lane = iota((BLOCK, b - a), 1) + a
            q = q_s[slot, :, a:b]
            q = jnp.where((lane >= lo) & (lane < hi), q, jnp.zeros_like(q))
            raw = dot(q, k_s[slot, :, a:b], NT)
            raw_s[h] = jnp.clip(raw * (1.0 / head_dim**0.5), -5.0, 5.0)

        def pair(g, _):
            def rows(side):
                return pl.ds(pl.multiple_of(g * (2 * GROUP) + side * GROUP, GROUP), GROUP)

            def both(f):
                return jnp.concatenate([f(0), f(1)], axis=1)

            edge2 = both(lambda side: edge_ref[0, :, rows(side), :].reshape(CH * GROUP, BLOCK))
            mix = dot(mix_map[...], edge2)
            bias, gate = mix[: HEADS * GROUP], mix[HEADS * GROUP :]
            score = both(lambda side: raw_s[:, rows(side), :].reshape(HEADS * GROUP, BLOCK)) + bias
            expo = jnp.exp(score)
            weight = (expo / (1.0 + jnp.exp(-gate))).astype(BF16)
            expo = expo.astype(BF16)
            for side in range(2):
                part = slice(side * BLOCK, (side + 1) * BLOCK)
                weight_s[:, rows(side), :] = weight[:, part].reshape(HEADS, GROUP, BLOCK)
                expo_s[:, rows(side), :] = expo[:, part].reshape(HEADS, GROUP, BLOCK)
            score = score.astype(BF16)
            mixed_s[...] = dot(out_map[...], jnp.concatenate([score, score], axis=0))
            for side in range(2):
                part = slice(side * BLOCK, (side + 1) * BLOCK)
                total = jnp.zeros((GROUP, BLOCK), F32)
                for c in range(CH):
                    m = mixed_s[c * GROUP : (c + 1) * GROUP, part] + edge_ref[0, c, rows(side), :].astype(F32)
                    mixed_s[c * GROUP : (c + 1) * GROUP, part] = m
                    total += m * m
                scale = lax.rsqrt(total * (1.0 / CH) + 1e-5)
                for c in range(CH):
                    m = mixed_s[c * GROUP : (c + 1) * GROUP, part]
                    out_ref[0, c, rows(side), :] = (m * (scale * gain_ref[c])).astype(BF16)
            return 0

        lax.fori_loop(0, BLOCK // (2 * GROUP), pair, 0)

        for m in range(tiles):
            heads = range(m * 128 // head_dim, (m * 128 + 127) // head_dim + 1)
            v = v_s[slot, :, m * 128 : (m + 1) * 128]
            lane = iota((BLOCK, 128), 1) + m * 128
            weights = jnp.concatenate([weight_s[h] for h in heads], axis=1)
            values = jnp.concatenate(
                [jnp.where(lane // head_dim == h, v, jnp.zeros_like(v)) for h in heads], axis=0
            )
            numer_ref[0, :, m * 128 : (m + 1) * 128] = dot(weights, values).astype(BF16)
        ones = where01(iota((HEADS, HEADS * BLOCK), 0) == iota((HEADS, HEADS * BLOCK), 1) // BLOCK)
        expo_all = jnp.concatenate([expo_s[h] for h in range(HEADS)], axis=1)
        denom_ref[0] = dot(ones, expo_all, NT)


def tile_call(count, gain_edge, dest, src, w_query, w_key, w_value, w_bias, w_gate, w_out, edges):
    slots, _, width = dest.shape
    vm = pl.BlockSpec(memory_space=pltpu.VMEM)
    sm = pl.BlockSpec(memory_space=pltpu.SMEM)
    edge_spec = pl.BlockSpec((1, CH, BLOCK, BLOCK), lambda s: (s, 0, 0, 0))
    return pl.pallas_call(
        tile_kernel,
        grid=(slots,),
        in_specs=[sm, sm] + [vm] * 8 + [edge_spec],
        out_specs=[
            pl.BlockSpec((1, BLOCK, width), lambda s: (s, 0, 0)),
            pl.BlockSpec((1, HEADS, BLOCK), lambda s: (s, 0, 0)),
            edge_spec,
        ],
        out_shape=[
            jax.ShapeDtypeStruct((slots, BLOCK, width), BF16),
            jax.ShapeDtypeStruct((slots, HEADS, BLOCK), F32),
            jax.ShapeDtypeStruct(edges.shape, BF16),
        ],
        scratch_shapes=[
            pltpu.VMEM((slots, BLOCK, width), BF16),
            pltpu.VMEM((slots, BLOCK, width), BF16),
            pltpu.VMEM((slots, BLOCK, width), BF16),
            pltpu.VMEM((2 * HEADS * GROUP, CH * GROUP), BF16),
            pltpu.VMEM((CH * GROUP, 2 * HEADS * GROUP), BF16),
            pltpu.VMEM((HEADS, BLOCK, BLOCK), F32),
            pltpu.VMEM((HEADS, BLOCK, BLOCK), BF16),
            pltpu.VMEM((HEADS, BLOCK, BLOCK), BF16),
            pltpu.VMEM((CH * GROUP, 2 * BLOCK), F32),
        ],
        compiler_params=pltpu.CompilerParams(vmem_limit_bytes=48 * 1024 * 1024),
        name="tile_work",
    )(count, gain_edge, dest, src, w_query, w_key, w_value, w_bias, w_gate, w_out, edges)


def on_device(
    nodes,
    w_query,
    w_key,
    w_value,
    w_out,
    w_edge_gate,
    w_edge_bias,
    w_edge_out,
    gain_node,
    gain_edge,
    edges,
    tile_list,
    tile_count,
):
    own_rows, width = nodes.shape
    head_dim = width // HEADS
    n_col = lax.axis_size("col")
    sources = lax.all_gather(nodes, "row", axis=0, tiled=True)
    dests = lax.all_gather(nodes, "col", axis=0, tiled=True)
    src_blocks = sources.shape[0] // BLOCK
    tiles = tile_list[0, 0]
    slots = tiles.shape[0]
    dest_id = tiles // src_blocks
    src_id = tiles % src_blocks
    dest = jnp.stack([lax.dynamic_slice_in_dim(dests, dest_id[s] * BLOCK, BLOCK, 0) for s in range(slots)])
    src = jnp.stack([lax.dynamic_slice_in_dim(sources, src_id[s] * BLOCK, BLOCK, 0) for s in range(slots)])
    numer, denom, edges_out = tile_call(
        tile_count.reshape(1),
        gain_edge,
        dest,
        src,
        w_query,
        w_key,
        w_value,
        w_edge_bias,
        w_edge_gate,
        w_edge_out,
        edges[0, 0],
    )
    dest_blocks = dests.shape[0] // BLOCK
    numer_all = jnp.zeros((dest_blocks, BLOCK, width), BF16)
    denom_all = jnp.zeros((dest_blocks, HEADS, BLOCK), F32)
    for s in range(slots):
        numer_all = lax.dynamic_update_slice(numer_all, numer[s : s + 1], (dest_id[s], 0, 0))
        denom_all = lax.dynamic_update_slice(denom_all, denom[s : s + 1], (dest_id[s], 0, 0))
    numer = lax.psum_scatter(numer_all, "col", scatter_dimension=0, tiled=True).astype(F32)
    denom = lax.psum_scatter(denom_all, "col", scatter_dimension=0, tiled=True)
    denom = denom.transpose(0, 2, 1).reshape(own_rows, HEADS, 1)
    numer = numer.reshape(own_rows, HEADS, head_dim)
    attended = jnp.where(denom > 0.0, numer / jnp.where(denom > 0.0, denom, 1.0), 0.0)
    attended = attended.reshape(own_rows, width).astype(BF16)
    mixed = nodes.astype(F32) + jnp.dot(attended, w_out, preferred_element_type=F32)
    square_mean = jnp.mean(mixed * mixed, axis=1, keepdims=True)
    nodes_out = (mixed * lax.rsqrt(square_mean + 1e-05) * gain_node).astype(BF16)
    return (nodes_out, edges_out[None, None])


def solution(mesh):
    return jax.shard_map(
        on_device,
        mesh=mesh,
        in_specs=(
            P(("row", "col"), None),
            *[P()] * 9,
            P("row", "col", None, None, None, None),
            P("row", "col", None),
            P("row", "col"),
        ),
        out_specs=(P(("row", "col"), None), P("row", "col", None, None, None, None)),
        check_vma=False,
    )
```

time: 323 us -> 234 us (0.72)
  matrix products: 58.3 us -> 0.77 us
  waiting for transfers between devices: 112 us -> 168 us
  local copies, waits for them, and re-layouts: 62.8 us -> 13 us
  other arithmetic: 36.7 us -> 3.91 us
  blocking collectives: 23.5 us -> 0 us
  Pallas kernels: 0 us -> 17.7 us
  between operations: 23.2 us -> 27.5 us
    dot_general x19 -> x1, matrix products: 58.3 us -> 0.77 us  [on_device(): jnp.dot(attended, w_out, preferred_element_type=F32)]
    reduce_scatter x0 -> x1, waiting for transfers between devices: none -> 38.8 us  [on_device(): lax.psum_scatter(numer_all, 'col', scatter_dimension=0, tiled=True)]
    unnamed x3 -> x5, waiting for transfers between devices: 0.05 us -> 28.6 us
    unnamed x57 -> x30, local copies, waits for them, and re-layouts: 31.5 us -> 3.87 us
    psum x1 -> x0, blocking collectives: 23.5 us -> none  [on_device(): lax.psum(denom.astype(jnp.bfloat16), 'col').astype(jnp.float32)]
    another operation x1 -> x2, other arithmetic: 23.5 us -> 0.2 us  [the longest x1 0.1 us: on_device(): jnp.stack([lax.dynamic_slice_in_dim(dests, dest_id[s] * BLOCK, BLOCK, 0)...]
    pallas_call x0 -> x1, Pallas kernels: none -> 17.7 us  [tile_call(): pl.pallas_call(tile_kernel, grid=(slots,), in_specs=[sm, sm] + [vm] * 8 +...]
    slice x7 -> x1, local copies, waits for them, and re-layouts: 13.7 us -> 0.68 us  [on_device(): src_id[s] * BLOCK]
  transfers between devices with their start and end apart: 3 -> 4, of which waited for: 1 -> 4; matrix products, arithmetic and copies ran while one was open for 38% -> 4% of each run, Pallas kernels for 0% -> 0%
where the time goes in v1:
time: 234 us; the launch traced here: 231 us
  waiting for transfers between devices  168 us (72%)
  between operations  27.5 us (12%)
  Pallas kernels  17.7 us (8%)
  local copies, waits for them, and re-layouts  13 us (6%)
  other arithmetic  3.91 us (2%)
    all_gather x1, waiting for transfers between devices, on_device(): sources = lax.all_gather(nodes, 'row', axis=0, tiled=True)  75.8 us
    reduce_scatter x1, waiting for transfers between devices, on_device(): lax.psum_scatter(numer_all, 'col', scatter_dimension=0, tiled=True)  38.8 us
    unnamed x5, waiting for transfers between devices  28.6 us
    all_gather x1, waiting for transfers between devices, on_device(): dests = lax.all_gather(nodes, 'col', axis=0, tiled=True)  24.8 us
    pallas_call x1, Pallas kernels, tile_call(): pl.pallas_call(tile_kernel, grid=(slots,), in_specs=[sm, sm] + [vm] * 8 +...  17.7 us
  transfers between devices with their start and end apart: 4, of which 4 were waited for; matrix products, arithmetic and copies ran while one was open for 4% of the time, Pallas kernels for 0%

profile of v1, /device:TPU:1, one launch (start us, length us, event | category | flops | bytes accessed | tf_op | source)
XLA Modules:
  0.0 231.0 jit_solution(16127202657769468657)
XLA Ops:
  7.2 0.0 copy-start
  7.2 0.0 all-gather.3.cloned.1.call-start
  7.3 0.7 all-gather.3.cloned.1.call-update
  7.9 0.0 all-gather.5.cloned.1.call-start
  8.0 0.7 all-gather.5.cloned.1.call-update
  8.7 0.0 reduce-scatter.7.cloned.1.call-start
  8.8 0.7 fusion.3
  19.7 0.0 copy-done.11
  19.7 0.1 copy.24.wb_ref
  19.8 0.0 copy-done.12
  19.8 0.1 copy.25.wg_ref
  23.2 24.8 %all-gather.3.cloned.1.call-done = bf16[3072,768]{1,0:T(8,128)(2,1)} async-done(((bf16[384,768]{1,0:T(8,128)(2,1)}), bf16[3072,768]{1,0:T(8,128)(2,1)}) %all-gather.3.cloned.1.call-update) | async-done | bytes 4718608 | tf_op jit(solution)/shard_map/all_gather | solution.py:211
  48.0 1.3 dynamic-slice_bitcast_fusion.7
  49.2 0.0 copy-start.3
  49.2 0.1 pad_maximum_fusion.dest_ref
  49.4 75.8 %all-gather.5.cloned.1.call-done = bf16[6144,768]{1,0:T(8,128)(2,1)} async-done(((bf16[384,768]{1,0:T(8,128)(2,1)}), bf16[6144,768]{1,0:T(8,128)(2,1)}) %all-gather.5.cloned.1.call-update) | async-done | bytes 9437200 | tf_op jit(solution)/shard_map/all_gather | solution.py:210
  125.1 1.4 dynamic-slice_bitcast_fusion.3
  126.5 0.0 copy-start.1
  126.5 0.0 copy-start.6
  126.5 0.0 copy-start.7
  126.5 0.1 pad_maximum_fusion.1.src_ref
  126.7 0.1 copy-done.2
  126.8 1.1 copy-done.1
  127.8 17.7 %tile_work.1 = (bf16[4,128,768]{2,1,0:T(8,128)(2,1)S(1)}, f32[4,8,128]{2,1,0:T(8,128)S(1)}, bf16[4,64,128,128]{3,2,1,0:T(8,128)(2,1)}) custom-call(s32[1]{0:T(128)} %bitcast.57.count_ref, f32[64]{0:T(128)S(1)} %copy-done.7, bf16[4,128,768]{2,1,0:T(8,128)(2,1)S(1)} %pad_maximum_fusion.dest_ref, bf16[4,128,768]{2,1,0:T(8,128)(2,1)S(1)} %pad_maximum_fusion.1.src_ref, ...), custom_call_target="tpu_custom_call" | custom-call | tf_op jit(solution)/shard_map/tile_work/pallas_call | solution.py:162
  145.6 0.9 copy-done.4
  146.5 0.0 copy-start.9
  146.5 0.6 copy-done.9
  147.2 0.0 reduce-scatter.7.cloned.1.call-update
  147.2 0.0 reduce-scatter.5.cloned.1.call-start
  147.2 0.0 copy-start.5
  147.2 2.7 %broadcast_in_dim.32 = bf16[24,128,768]{2,1,0:T(8,128)(2,1)} broadcast(bf16[]{:T(256)} %constant.43.clone.1), dimensions={} | broadcast | bytes 4718594 | tf_op jit(solution)/shard_map/broadcast_in_dim | solution.py:233
  149.9 0.7 slice_dynamic-update-slice_fusion.3
  150.6 0.7 slice_dynamic-update-slice_fusion.2
  151.3 0.7 slice_dynamic-update-slice_fusion.1
  152.0 0.7 slice_dynamic-update-slice_fusion
  152.6 0.0 reduce-scatter.5.cloned.1.call-update
  152.7 27.2 %reduce-scatter.7.cloned.1.call-done = f32[3,8,128]{2,1,0:T(8,128)} async-done(((f32[24,8,128]{2,1,0:T(8,128)}), f32[3,8,128]{2,1,0:T(8,128)}) %reduce-scatter.7.cloned.1.call-update) | async-done | bytes 12304
  179.8 0.7 bitcast_compare_fusion
  180.5 0.7 bitcast_select_fusion
  181.3 38.8 %reduce-scatter.5.cloned.1.call-done = bf16[3,128,768]{2,1,0:T(8,128)(2,1)} async-done(((bf16[24,128,768]{2,1,0:T(8,128)(2,1)}), bf16[3,128,768]{2,1,0:T(8,128)(2,1)}) %reduce-scatter.5.cloned.1.call-update) | async-done | bytes 589840 | tf_op jit(solution)/shard_map/reduce_scatter | solution.py:238
  220.1 1.1 bitcast_convert_fusion
  221.2 0.4 copy.26
  221.6 0.0 copy-start.8
  221.6 0.1 fusion.1
  221.8 0.9 copy-done.8
  222.7 0.8 multiply_reduce_fusion
  223.5 0.0 copy-done.10
  223.5 1.0 multiply_convert_fusion
  (19 shorter events, 0.1 us)
Async XLA Ops:
  7.2 214.6 %copy-start = (bf16[768,768]{1,0:T(8,128)(2,1)S(1)}, bf16[768,768]{1,0:T(8,128)(2,1)}, u32[]{:S(2)}) copy-start(bf16[768,768]{1,0:T(8,128)(2,1)} %param.17) | copy-start | bytes 3538948
  7.2 1.6 copy-start.13
  7.2 12.5 %copy-start.11 = (bf16[64,8]{0,1:T(8,128)(2,1)S(1)}, bf16[64,8]{0,1:T(8,128)(2,1)}, u32[]{:S(2)}) copy-start(bf16[64,8]{0,1:T(8,128)(2,1)} %param.19) | copy-start | bytes 3076
  7.2 12.6 %copy-start.12 = (bf16[64,8]{0,1:T(8,128)(2,1)S(1)}, bf16[64,8]{0,1:T(8,128)(2,1)}, u32[]{:S(2)}) copy-start(bf16[64,8]{0,1:T(8,128)(2,1)} %param.18) | copy-start | bytes 3076
  7.2 40.7 %all-gather.3.cloned.1.call-start = ((), (), s32[]{:S(2)}) async-start(), calls=%async_computation.2 | async-start | bytes 5308416 | tf_op jit(solution)/shard_map/all_gather | solution.py:211
  7.9 117.2 %all-gather.5.cloned.1.call-start = ((), (), s32[]{:S(2)}) async-start(), calls=%async_computation.3 | async-start | bytes 10027008 | tf_op jit(solution)/shard_map/all_gather | solution.py:210
  8.7 171.1 %reduce-scatter.7.cloned.1.call-start = ((), (), s32[]{:S(2)}) async-start(), calls=%async_computation.5 | async-start | bytes 110592
  49.2 77.4 %copy-start.3 = (bf16[768,768]{1,0:T(8,128)(2,1)S(1)}, bf16[768,768]{1,0:T(8,128)(2,1)}, u32[]{:S(2)}) copy-start(bf16[768,768]{1,0:T(8,128)(2,1)} %wv_ref.1) | copy-start | bytes 3538948
  125.1 1.6 copy-start.2
  126.5 1.3 copy-start.1
  126.5 1.3 copy-start.6
  126.5 1.3 copy-start.7
  145.6 0.9 copy-start.4
  146.5 0.6 copy-start.9
  147.2 72.9 %reduce-scatter.5.cloned.1.call-start = ((), (), s32[]{:S(2)}) async-start(), calls=%async_computation.4 | async-start | bytes 5308416 | tf_op jit(solution)/shard_map/reduce_scatter | solution.py:238
  147.2 2.7 %copy-start.5 = (bf16[4,128,768]{2,1,0:T(8,128)(2,1)S(1)}, bf16[4,128,768]{2,1,0:T(8,128)(2,1)}, u32[]{:S(2)}) copy-start(bf16[4,128,768]{2,1,0:T(8,128)(2,1)} %copy-done.4) | copy-start | bytes 2359300
  221.6 1.1 copy-start.8
  222.7 0.8 copy-start.10
Sparse Core Ops, SparseCore 0:
  9.7 38.1 all-gather.2
  50.1 74.9 all-gather.4
  147.3 32.4 reduce-scatter.6
  182.2 37.8 reduce-scatter.4

commit v2 on v1

--- a/solution.py
+++ b/solution.py
@@ -189,6 +189,428 @@
     )(count, gain_edge, dest, src, w_query, w_key, w_value, w_bias, w_gate, w_out, edges)
 
 
+NX, NY, NZ = 4, 4, 4
+PIECES = 6
+MESH = pl.DeviceIdType.MESH
+
+
+def place():
+    row, col = lax.axis_index("row"), lax.axis_index("col")
+    x, y, z, core = row // NY, row % NY, col // 2, col % 2
+
+    def on_x(k):
+        return (lax.rem(x + k, NX) * NY + y, col)
+
+    def on_y(k):
+        return (x * NY + lax.rem(y + k, NY), col)
+
+    def on_z(k):
+        return (row, lax.rem(z + k, NZ) * 2 + core)
+
+    return x, y, z, core, on_x, on_y, on_z, (row, z * 2 + 1 - core)
+
+
+def greet(peers):
+    barrier = pltpu.get_barrier_semaphore()
+    for peer in peers:
+        pl.semaphore_signal(barrier, inc=1, device_id=peer, device_id_type=MESH)
+    pl.semaphore_wait(barrier, len(peers))
+
+
+def remote(src, dst, send_sem, recv_sem, peer):
+    return pltpu.make_async_remote_copy(
+        src_ref=src, dst_ref=dst, send_sem=send_sem, recv_sem=recv_sem, device_id=peer, device_id_type=MESH
+    )
+
+
+def gather_kernel(
+    tile_ref,
+    nodes_ref,
+    src_out,
+    dest_out,
+    sib_out,
+    pool_y,
+    pool_x,
+    pool_z,
+    fill_send,
+    fill_recv,
+    core_send,
+    core_recv,
+    meta_own,
+    meta_vmem,
+    meta,
+    ring_send_sem,
+    ring_recv_sem,
+    fill_send_sem,
+    fill_recv_sem,
+    meta_send_sem,
+    meta_recv_sem,
+    core_sem,
+    local_sem,
+):
+    x, y, z, core, on_x, on_y, on_z, sibling = place()
+    width = nodes_ref.shape[-1]
+    half = width // 2
+    per_dev = PIECES // 2
+    src_blocks = NX * NY * per_dev
+    slots = src_out.shape[0]
+    greet([on_x(1), on_x(3), on_x(2), on_y(1), on_y(3), on_y(2), on_z(1), on_z(3), sibling])
+
+    lane = iota(meta_own.shape, 1)
+    words = jnp.zeros(meta_own.shape, jnp.int32)
+    for s in range(slots):
+        words = jnp.where(lane == s, tile_ref[s] % src_blocks, words)
+        words = jnp.where(lane == slots + s, tile_ref[s] // src_blocks, words)
+    meta_own[...] = words
+    meta_copies = []
+    for k, (peer, there) in enumerate(
+        [(on_x(3), 0), (on_x(1), 1), (on_x(2), 2), (on_y(3), 3), (on_y(1), 4), (on_y(2), 5), (sibling, 6)]
+    ):
+        copy = remote(meta_own, meta_vmem.at[there], meta_send_sem.at[there], meta_recv_sem.at[there], peer)
+        copy.start()
+        meta_copies.append(copy)
+
+    rings = [
+        (pool_y, y, on_y, 0, half),
+        (pool_x, x, on_x, half, width),
+        (pool_z, z, on_z, 0, width),
+    ]
+    low, high = pl.ds(0, PIECES // 2), pl.ds(PIECES // 2, PIECES // 2)
+    ring_copies = []
+    for r, (pool, pos, on, a, b) in enumerate(rings):
+        copies = {}
+        for step in range(2):
+            for way, peer in ((0, on(1)), (1, on(3))):
+                part = step if way == 0 else 1 - step
+                copies[way, step] = remote(
+                    nodes_ref.at[(low, high)[part], :, a:b],
+                    pool.at[pl.ds(pos * PIECES + part * (PIECES // 2), PIECES // 2)],
+                    ring_send_sem.at[r, way, step],
+                    ring_recv_sem.at[r, way, step],
+                    peer,
+                )
+        ring_copies.append(copies)
+    for step in range(2):
+        for r in range(3):
+            for way in range(2):
+                ring_copies[r][way, step].start()
+    for pool, pos, on, a, b in rings:
+        pool[pl.ds(pos * PIECES, PIECES)] = nodes_ref[:, :, a:b]
+
+    for r, (pool, pos, on, a, b) in enumerate(rings):
+        for way, peer, owner in ((0, on(1), lax.rem(pos + 3, 4)), (1, on(3), lax.rem(pos + 1, 4))):
+            ring_copies[r][way, 0].wait_recv()
+            here = pool.at[pl.ds(owner * PIECES + way * (PIECES // 2), PIECES // 2)]
+            ring_copies[r][way, 2] = remote(
+                here, here, ring_send_sem.at[r, way, 2], ring_recv_sem.at[r, way, 2], peer
+            )
+            ring_copies[r][way, 2].start()
+
+    for copy in meta_copies:
+        copy.wait_recv()
+    to_smem = pltpu.make_async_copy(meta_vmem, meta, local_sem)
+    to_smem.start()
+    to_smem.wait()
+    sib_out[...] = meta_vmem[6]
+
+    def source(who, s):
+        block = tile_ref[s] % src_blocks if who is None else meta[who, 0, s]
+        t, o = block // per_dev, block % per_dev
+        return t // NY, t % NY, o
+
+    def along_x(who, s):
+        bx, by, o = source(who, s)
+        return bx, by * per_dev + o
+
+    def along_y(who, s):
+        bx, by, o = source(who, s)
+        return by, bx * per_dev + o
+
+    def load(pool, block):
+        return pool[pl.ds(block * 2, 2)]
+
+    fills = [(pool_y, x, on_x, along_x, (0, 1, 2)), (pool_x, y, on_y, along_y, (3, 4, 5))]
+    fill_copies = []
+
+    def send_fill(f, way, part, peer):
+        copy = remote(
+            fill_send.at[f, way, part],
+            fill_recv.at[f, way, part],
+            fill_send_sem.at[f, way, part],
+            fill_recv_sem.at[f, way, part],
+            peer,
+        )
+        copy.start()
+        return copy
+
+    for f, (pool, pos, on, along, (plus, minus, far)) in enumerate(fills):
+        for way in range(2):
+            for step in (1, 2):
+                ring_copies[f][way, step].wait_recv()
+        copies = {}
+        for part, who_of in ((0, (far, far)), (1, (plus, minus))):
+            for way, peer in ((0, on(1)), (1, on(3))):
+                first = 2 * (way if part == 0 else 1 - way)
+                for k in range(2):
+                    fill_send[f, way, part, k] = load(pool, along(who_of[way], first + k)[1])
+                copies[way, part] = send_fill(f, way, part, peer)
+        fill_copies.append(copies)
+    for f, (pool, pos, on, along, (plus, minus, far)) in enumerate(fills):
+        copies = fill_copies[f]
+        for way, peer, who in ((0, on(1), plus), (1, on(3), minus)):
+            copies[way, 0].wait_recv()
+            for k in range(2):
+                at, block = along(who, 2 * way + k)
+                fill_send[f, way, 2, k] = jnp.where(at == pos, load(pool, block), fill_recv[f, way, 0, k])
+            copies[way, 2] = send_fill(f, way, 2, peer)
+
+    for way in range(2):
+        for step in (1, 2):
+            ring_copies[2][way, step].wait_recv()
+
+    def dest(who, s):
+        block = tile_ref[s] // src_blocks if who is None else meta[who, 0, slots + s]
+        owner, o = block // per_dev, block % per_dev
+        return owner % 2, (owner // 2) * per_dev + o
+
+    for s in range(slots):
+        core_send[s] = load(pool_z, dest(6, s)[1])
+    core_copy = remote(core_send, core_recv, core_sem.at[0], core_sem.at[1], sibling)
+    core_copy.start()
+
+    for f, (pool, pos, on, along, (plus, minus, far)) in enumerate(fills):
+        copies = fill_copies[f]
+        for way in range(2):
+            for part in (1, 2):
+                copies[way, part].wait_recv()
+        for s in range(slots):
+            at, block = along(None, s)
+            own = load(pool, block)
+            k = s % 2
+            if s < 2:
+                near, other = fill_recv[f, 1, 1, k], fill_recv[f, 0, 2, k]
+                is_near = at == lax.rem(pos + 1, 4)
+            else:
+                near, other = fill_recv[f, 0, 1, k], fill_recv[f, 1, 2, k]
+                is_near = at == lax.rem(pos + 3, 4)
+            src_out[s, :, :, f * half : (f + 1) * half] = jnp.where(
+                at == pos, own, jnp.where(is_near, near, other)
+            )
+    core_copy.wait_recv()
+    for s in range(slots):
+        at, block = dest(None, s)
+        dest_out[s] = jnp.where(at == core, load(pool_z, block), core_recv[s])
+    core_copy.wait_send()
+    for copy in meta_copies:
+        copy.wait_send()
+    for copies in ring_copies + fill_copies:
+        for copy in copies.values():
+            copy.wait_send()
+
+
+def gather_call(tiles, nodes):
+    rows, width = nodes.shape
+    slots = tiles.shape[0]
+    piece = rows // PIECES
+    half = width // 2
+    vm = pl.BlockSpec(memory_space=pltpu.VMEM)
+    sm = pl.BlockSpec(memory_space=pltpu.SMEM)
+    dma = pltpu.SemaphoreType.DMA
+    blocks = jax.ShapeDtypeStruct((slots, 2, piece, width), BF16)
+    src, dest, sib = pl.pallas_call(
+        gather_kernel,
+        in_specs=[sm, vm],
+        out_specs=[vm, vm, vm],
+        out_shape=[blocks, blocks, jax.ShapeDtypeStruct((8, 128), jnp.int32)],
+        scratch_shapes=[
+            pltpu.VMEM((4 * PIECES, piece, half), BF16),
+            pltpu.VMEM((4 * PIECES, piece, half), BF16),
+            pltpu.VMEM((4 * PIECES, piece, width), BF16),
+            pltpu.VMEM((2, 2, 3, 2, 2, piece, half), BF16),
+            pltpu.VMEM((2, 2, 3, 2, 2, piece, half), BF16),
+            pltpu.VMEM((slots, 2, piece, width), BF16),
+            pltpu.VMEM((slots, 2, piece, width), BF16),
+            pltpu.VMEM((8, 128), jnp.int32),
+            pltpu.VMEM((7, 8, 128), jnp.int32),
+            pltpu.SMEM((7, 8, 128), jnp.int32),
+            dma((3, 2, 3)),
+            dma((3, 2, 3)),
+            dma((2, 2, 3)),
+            dma((2, 2, 3)),
+            dma((7,)),
+            dma((7,)),
+            dma((2,)),
+            dma,
+        ],
+        compiler_params=pltpu.CompilerParams(
+            collective_id=0, has_side_effects=True, vmem_limit_bytes=48 * 1024 * 1024
+        ),
+        name="gather_blocks",
+    )(tiles, nodes.reshape(PIECES, piece, width))
+    return src.reshape(slots, BLOCK, width), dest.reshape(slots, BLOCK, width), sib[0]
+
+
+def reduce_kernel(
+    tile_ref,
+    sib_ref,
+    numer_ref,
+    denom_ref,
+    nodes_ref,
+    w_ref,
+    gain_ref,
+    out_ref,
+    sib_numer,
+    send,
+    recv,
+    den_send,
+    den_recv,
+    total,
+    sib_sem,
+    send_sem,
+    recv_sem,
+    den_send_sem,
+    den_recv_sem,
+):
+    x, y, z, core, on_x, on_y, on_z, sibling = place()
+    row, col = lax.axis_index("row"), lax.axis_index("col")
+    n_col = 2 * NZ
+    slots = denom_ref.shape[0]
+    src_blocks = NX * NY * (PIECES // 2)
+    per_dev = PIECES // 2
+    piece, width = numer_ref.shape[1:]
+    head_dim = width // HEADS
+    others = [(row, lax.rem(col + k, n_col)) for k in range(1, n_col)]
+    greet(others)
+    sib_copy = remote(numer_ref, sib_numer, sib_sem.at[0], sib_sem.at[1], sibling)
+    sib_copy.start()
+    mine = [tile_ref[s] // src_blocks for s in range(slots)]
+    theirs = [sib_ref[slots + s] for s in range(slots)]
+
+    def find(ids, a):
+        index, found = jnp.int32(0), jnp.int32(0)
+        for s in range(slots):
+            index = jnp.where(ids[s] == a, s, index)
+            found = jnp.where(ids[s] == a, 1, found)
+        return index, found
+
+    def denom_of(owner, o):
+        index, found = find(mine, owner * per_dev + o)
+        d = denom_ref[index]
+        return jnp.where(found > 0, d, jnp.zeros_like(d))
+
+    den_copies = []
+    for k in range(1, n_col):
+        for o in range(per_dev):
+            den_send[k, o] = denom_of(lax.rem(col + k, n_col), o)
+        copy = remote(den_send.at[k], den_recv.at[k], den_send_sem.at[k], den_recv_sem.at[k], others[k - 1])
+        copy.start()
+        den_copies.append(copy)
+    sib_copy.wait_recv()
+
+    def chunk(at, p):
+        a = (at * 2 + core) * per_dev + p // 2
+        i, f = find(mine, a)
+        j, g = find(theirs, a)
+        u = numer_ref[i * 2 + p % 2].astype(F32)
+        v = sib_numer[j * 2 + p % 2].astype(F32)
+        return jnp.where(f > 0, u, jnp.zeros_like(u)) + jnp.where(g > 0, v, jnp.zeros_like(v))
+
+    half = PIECES // 2
+    copies = {}
+
+    def start(way, part):
+        copies[way, part] = remote(
+            send.at[way, part],
+            recv.at[way, part],
+            send_sem.at[way, part],
+            recv_sem.at[way, part],
+            on_z(1 + 2 * way),
+        )
+        copies[way, part].start()
+
+    for part in range(2):
+        for way in range(2):
+            at = lax.rem(z + (2 if part == 0 else 1 + 2 * way), NZ)
+            first = half * (way if part == 0 else 1 - way)
+            for k in range(half):
+                send[way, part, k] = chunk(at, first + k).astype(BF16)
+            start(way, part)
+    for way in range(2):
+        at = lax.rem(z + 1 + 2 * way, NZ)
+        copies[way, 0].wait_recv()
+        for k in range(half):
+            send[way, 2, k] = (chunk(at, half * way + k) + recv[way, 0, k].astype(F32)).astype(BF16)
+        start(way, 2)
+    for p in range(PIECES):
+        total[p] = chunk(z, p)
+    for copy in den_copies:
+        copy.wait_recv()
+    expand = where01(iota((2 * HEADS, width), 0) % HEADS == iota((2 * HEADS, width), 1) // head_dim)
+    scales = []
+    for o in range(per_dev):
+        d = denom_of(col, o)
+        for k in range(1, n_col):
+            d += den_recv[k, o]
+        inverse = jnp.where(d > 0.0, 1.0 / jnp.where(d > 0.0, d, 1.0), 0.0)
+        upper = inverse.astype(BF16)
+        lower = (inverse - upper.astype(F32)).astype(BF16)
+        both = jnp.concatenate([upper.astype(F32), lower.astype(F32)], axis=0).astype(BF16)
+        scales.append(dot(both, expand, (((0,), (0,)), ((), ()))))
+    for part in (1, 2):
+        for way in range(2):
+            copies[way, part].wait_recv()
+    for o in range(per_dev):
+        parts = []
+        for p in (2 * o, 2 * o + 1):
+            k = p % half
+            if p < half:
+                parts.append(total[p] + recv[0, 2, k].astype(F32) + recv[1, 1, k].astype(F32))
+            else:
+                parts.append(total[p] + recv[0, 1, k].astype(F32) + recv[1, 2, k].astype(F32))
+        numer = jnp.concatenate(parts, axis=0)
+        attended = (numer * scales[o]).astype(BF16)
+        rows = slice(o * BLOCK, (o + 1) * BLOCK)
+        mixed = nodes_ref[rows].astype(F32) + dot(attended, w_ref[...])
+        mean = jnp.mean(mixed * mixed, axis=1, keepdims=True)
+        out_ref[rows] = (mixed * lax.rsqrt(mean + 1e-05) * gain_ref[...]).astype(BF16)
+    sib_copy.wait_send()
+    for copy in den_copies + list(copies.values()):
+        copy.wait_send()
+
+
+def reduce_call(tiles, sib, numer, denom, nodes, w_out, gain_node):
+    slots, _, width = numer.shape
+    rows = nodes.shape[0]
+    piece = rows // PIECES
+    vm = pl.BlockSpec(memory_space=pltpu.VMEM)
+    sm = pl.BlockSpec(memory_space=pltpu.SMEM)
+    dma = pltpu.SemaphoreType.DMA
+    per_dev = PIECES // 2
+    return pl.pallas_call(
+        reduce_kernel,
+        in_specs=[sm, sm] + [vm] * 5,
+        out_specs=vm,
+        out_shape=jax.ShapeDtypeStruct((rows, width), BF16),
+        scratch_shapes=[
+            pltpu.VMEM((2 * slots, piece, width), BF16),
+            pltpu.VMEM((2, 3, per_dev, piece, width), BF16),
+            pltpu.VMEM((2, 3, per_dev, piece, width), BF16),
+            pltpu.VMEM((2 * NZ, per_dev, HEADS, BLOCK), F32),
+            pltpu.VMEM((2 * NZ, per_dev, HEADS, BLOCK), F32),
+            pltpu.VMEM((PIECES, piece, width), F32),
+            dma((2,)),
+            dma((2, 3)),
+            dma((2, 3)),
+            dma((2 * NZ,)),
+            dma((2 * NZ,)),
+        ],
+        compiler_params=pltpu.CompilerParams(
+            collective_id=1, has_side_effects=True, vmem_limit_bytes=48 * 1024 * 1024
+        ),
+        name="reduce_nodes",
+    )(tiles, sib, numer.reshape(2 * slots, piece, width), denom, nodes, w_out, gain_node.reshape(1, width))
+
+
 def on_device(
     nodes,
     w_query,
@@ -204,18 +626,8 @@
     tile_list,
     tile_count,
 ):
-    own_rows, width = nodes.shape
-    head_dim = width // HEADS
-    n_col = lax.axis_size("col")
-    sources = lax.all_gather(nodes, "row", axis=0, tiled=True)
-    dests = lax.all_gather(nodes, "col", axis=0, tiled=True)
-    src_blocks = sources.shape[0] // BLOCK
-    tiles = tile_list[0, 0]
-    slots = tiles.shape[0]
-    dest_id = tiles // src_blocks
-    src_id = tiles % src_blocks
-    dest = jnp.stack([lax.dynamic_slice_in_dim(dests, dest_id[s] * BLOCK, BLOCK, 0) for s in range(slots)])
-    src = jnp.stack([lax.dynamic_slice_in_dim(sources, src_id[s] * BLOCK, BLOCK, 0) for s in range(slots)])
+    tiles = tile_list.reshape(-1)
+    src, dest, sib = gather_call(tiles, nodes)
     numer, denom, edges_out = tile_call(
         tile_count.reshape(1),
         gain_edge,
@@ -229,21 +641,7 @@
         w_edge_out,
         edges[0, 0],
     )
-    dest_blocks = dests.shape[0] // BLOCK
-    numer_all = jnp.zeros((dest_blocks, BLOCK, width), BF16)
-    denom_all = jnp.zeros((dest_blocks, HEADS, BLOCK), F32)
-    for s in range(slots):
-        numer_all = lax.dynamic_update_slice(numer_all, numer[s : s + 1], (dest_id[s], 0, 0))
-        denom_all = lax.dynamic_update_slice(denom_all, denom[s : s + 1], (dest_id[s], 0, 0))
-    numer = lax.psum_scatter(numer_all, "col", scatter_dimension=0, tiled=True).astype(F32)
-    denom = lax.psum_scatter(denom_all, "col", scatter_dimension=0, tiled=True)
-    denom = denom.transpose(0, 2, 1).reshape(own_rows, HEADS, 1)
-    numer = numer.reshape(own_rows, HEADS, head_dim)
-    attended = jnp.where(denom > 0.0, numer / jnp.where(denom > 0.0, denom, 1.0), 0.0)
-    attended = attended.reshape(own_rows, width).astype(BF16)
-    mixed = nodes.astype(F32) + jnp.dot(attended, w_out, preferred_element_type=F32)
-    square_mean = jnp.mean(mixed * mixed, axis=1, keepdims=True)
-    nodes_out = (mixed * lax.rsqrt(square_mean + 1e-05) * gain_node).astype(BF16)
+    nodes_out = reduce_call(tiles, sib, numer, denom, nodes, w_out, gain_node)
     return (nodes_out, edges_out[None, None])
 
 

time: 234 us -> 94.5 us (0.40)
  waiting for transfers between devices: 168 us -> 0 us
  Pallas kernels: 17.7 us -> 82.7 us
  between operations: 27.5 us -> 1.35 us
  other arithmetic: 3.91 us -> 0 us
  local copies, waits for them, and re-layouts: 13 us -> 9.26 us
    all_gather x2 -> x0, waiting for transfers between devices: 101 us -> none  [the longest x1 75.8 us: on_device(): sources = lax.all_gather(nodes, 'row', axis=0, tiled=True)]
    pallas_call x0 -> x2, Pallas kernels: none -> 64.8 us  [the longest x1 33.5 us: gather_call(): pl.pallas_call(gather_kernel, in_specs=[sm, vm], out_specs=[vm, vm, vm],...]
    reduce_scatter x1 -> x0, waiting for transfers between devices: 38.8 us -> none  [on_device(): lax.psum_scatter(numer_all, 'col', scatter_dimension=0, tiled=True)]
    unnamed x5 -> x0, waiting for transfers between devices: 28.6 us -> none
    unnamed x30 -> x25, local copies, waits for them, and re-layouts: 3.87 us -> 9.25 us
    dynamic_update_slice x8 -> x0, local copies, waits for them, and re-layouts: 2.77 us -> none  [the longest x4 2.74 us: on_device(): lax.dynamic_update_slice(numer_all, numer[s:s + 1], (dest_id[s], 0, 0))]
    broadcast_in_dim x2 -> x0, local copies, waits for them, and re-layouts: 2.66 us -> none  [the longest x1 2.65 us: on_device(): numer_all = jnp.zeros((dest_blocks, BLOCK, width), BF16)]
    another operation x2 -> x0, local copies, waits for them, and re-layouts: 2.63 us -> none  [the longest x1 1.36 us: on_device(): jnp.stack([lax.dynamic_slice_in_dim(sources, src_id[s] * BLOCK, BLOCK, 0)...]
  transfers between devices with their start and end apart: 4 -> 0, of which waited for: 4 -> 0; matrix products, arithmetic and copies ran while one was open for 4% -> 0% of each run, Pallas kernels for 0% -> 0%
where the time goes in v2:
time: 94.5 us; the launch traced here: 93.3 us
  Pallas kernels  82.7 us (88%)
  local copies, waits for them, and re-layouts  9.26 us (10%)
  between operations  1.35 us (1%)
    pallas_call x1, Pallas kernels, gather_call(): pl.pallas_call(gather_kernel, in_specs=[sm, vm], out_specs=[vm, vm, vm],...  33.5 us
    pallas_call x1, Pallas kernels, reduce_call(): pl.pallas_call(reduce_kernel, in_specs=[sm, sm] + [vm] * 5, out_specs=vm,...  31.4 us
    pallas_call x1, Pallas kernels, tile_call(): pl.pallas_call(tile_kernel, grid=(slots,), in_specs=[sm, sm] + [vm] * 8 +...  17.9 us
    unnamed x25, local copies, waits for them, and re-layouts  9.25 us

profile of v2, /device:TPU:1, one launch (start us, length us, event | category | flops | bytes accessed | tf_op | source)
XLA Modules:
  0.0 93.3 jit_solution(13678895621614850239)
XLA Ops:
  0.6 0.0 copy-start
  0.6 1.1 %copy-done = bf16[384,768]{1,0:T(8,128)(2,1)S(1)} copy-done((bf16[384,768]{1,0:T(8,128)(2,1)S(1)}, bf16[384,768]{1,0:T(8,128)(2,1)}, u32[]{:S(2)}) %copy-start) | copy-done | bytes 589848
  1.7 0.0 copy-start.7
  1.7 0.7 copy-done.7
  2.4 33.5 %gather_blocks.1 = (bf16[4,2,64,768]{3,2,1,0:T(8,128)(2,1)S(1)}, bf16[4,2,64,768]{3,2,1,0:T(8,128)(2,1)S(1)}, s32[8,128]{1,0:T(8,128)S(1)}) custom-call(s32[4]{0:T(128)S(1)} %bitcast.15, bf16[6,64,768]{2,1,0:T(8,128)(2,1)S(1)} %bitcast.11), custom_call_target="tpu_custom_call" | custom-call | tf_op jit(solution)/shard_map/gather_blocks/pallas_call | solution.py:420
  36.5 0.8 copy.15.wb_ref
  37.3 0.8 copy.16.wg_ref
  38.1 0.0 copy-start.2
  38.1 1.3 %copy-done.2 = bf16[768,768]{1,0:T(8,128)(2,1)S(1)} copy-done((bf16[768,768]{1,0:T(8,128)(2,1)S(1)}, bf16[768,768]{1,0:T(8,128)(2,1)}, u32[]{:S(2)}) %copy-start.2) | copy-done | bytes 1179672
  39.3 0.0 copy-start.3
  39.3 1.3 %copy-done.3 = bf16[768,768]{1,0:T(8,128)(2,1)S(1)} copy-done((bf16[768,768]{1,0:T(8,128)(2,1)S(1)}, bf16[768,768]{1,0:T(8,128)(2,1)}, u32[]{:S(2)}) %copy-start.3) | copy-done | bytes 1179672
  40.6 0.0 copy-start.4
  40.6 1.3 %copy-done.4 = bf16[768,768]{1,0:T(8,128)(2,1)S(1)} copy-done((bf16[768,768]{1,0:T(8,128)(2,1)S(1)}, bf16[768,768]{1,0:T(8,128)(2,1)}, u32[]{:S(2)}) %copy-start.4) | copy-done | bytes 1179672
  41.9 0.0 copy-start.6
  41.9 0.7 copy-done.6
  42.6 0.0 copy-start.9
  42.6 0.7 copy-done.9
  43.2 0.0 copy-start.10
  43.2 0.0 copy-start.1
  43.2 0.0 copy-start.5
  43.2 0.0 copy-start.8
  43.2 17.9 %tile_work.1 = (bf16[4,128,768]{2,1,0:T(8,128)(2,1)S(1)}, f32[4,8,128]{2,1,0:T(8,128)S(1)}, bf16[4,64,128,128]{3,2,1,0:T(8,128)(2,1)}) custom-call(s32[1]{0:T(128)} %bitcast.10.count_ref, f32[64]{0:T(128)S(1)} %copy-done.9, bf16[4,128,768]{2,1,0:T(8,128)(2,1)S(1)} %bitcast.13, bf16[4,128,768]{2,1,0:T(8,128)(2,1)S(1)} %bitcast.12, ...), custom_call_target="tpu_custom_call" | custom-call | tf_op jit(solution)/shard_map/tile_work/pallas_call | solution.py:162
  61.1 0.0 copy-done.10
  61.1 0.0 copy-done.1
  61.1 0.0 copy-done.5
  61.1 0.0 copy-done.8
  61.1 31.4 %reduce_nodes.1 = bf16[384,768]{1,0:T(8,128)(2,1)S(1)} custom-call(s32[4]{0:T(128)S(1)} %bitcast.16, s32[128]{0:T(128)S(1)} %slice_bitcast_fusion.sib_ref, bf16[8,64,768]{2,1,0:T(8,128)(2,1)S(1)} %bitcast.14, f32[4,8,128]{2,1,0:T(8,128)S(1)} %get-tuple-element.12.denom_ref, bf16[384,768]{1,0:T(8,128)(2,1)S(1)} %copy-done.1, bf16[768,768]{1,0:T(8,128)(2,1)S(1)} %copy-done.5, ...), custom_call_target="tpu_custom_call" | custom-call | tf_op jit(solution)/shard_map/reduce_nodes/pallas_call | solution.py:589
  92.5 0.8 copy.19
  (2 shorter events, 0.0 us)
Async XLA Ops:
  0.6 1.1 %copy-start = (bf16[384,768]{1,0:T(8,128)(2,1)S(1)}, bf16[384,768]{1,0:T(8,128)(2,1)}, u32[]{:S(2)}) copy-start(bf16[384,768]{1,0:T(8,128)(2,1)} %nodes_ref.1) | copy-start | bytes 1769476
  1.7 0.7 copy-start.7
  38.1 1.3 %copy-start.2 = (bf16[768,768]{1,0:T(8,128)(2,1)S(1)}, bf16[768,768]{1,0:T(8,128)(2,1)}, u32[]{:S(2)}) copy-start(bf16[768,768]{1,0:T(8,128)(2,1)} %wq_ref.1) | copy-start | bytes 3538948
  39.3 1.3 %copy-start.3 = (bf16[768,768]{1,0:T(8,128)(2,1)S(1)}, bf16[768,768]{1,0:T(8,128)(2,1)}, u32[]{:S(2)}) copy-start(bf16[768,768]{1,0:T(8,128)(2,1)} %wk_ref.1) | copy-start | bytes 3538948
  40.6 1.3 %copy-start.4 = (bf16[768,768]{1,0:T(8,128)(2,1)S(1)}, bf16[768,768]{1,0:T(8,128)(2,1)}, u32[]{:S(2)}) copy-start(bf16[768,768]{1,0:T(8,128)(2,1)} %wv_ref.1) | copy-start | bytes 3538948
  41.9 0.7 copy-start.6
  42.6 0.7 copy-start.9
  43.2 17.9 %copy-start.10 = (f32[768]{0:T(1024)S(1)}, f32[768]{0:T(1024)}, u32[]{:S(2)}) copy-start(f32[768]{0:T(1024)} %param.21) | copy-start | bytes 9220
  43.2 17.9 %copy-start.1 = (bf16[384,768]{1,0:T(8,128)(2,1)S(1)}, bf16[384,768]{1,0:T(8,128)(2,1)}, u32[]{:S(2)}) copy-start(bf16[384,768]{1,0:T(8,128)(2,1)} %nodes_ref.1) | copy-start | bytes 1769476
  43.2 17.9 %copy-start.5 = (bf16[768,768]{1,0:T(8,128)(2,1)S(1)}, bf16[768,768]{1,0:T(8,128)(2,1)}, u32[]{:S(2)}) copy-start(bf16[768,768]{1,0:T(8,128)(2,1)} %w_ref.1) | copy-start | bytes 3538948
  43.2 17.9 %copy-start.8 = (s32[1,1,4]{2,1,0:T(1,128)S(1)}, s32[1,1,4]{2,1,0:T(1,128)}, u32[]{:S(2)}) copy-start(s32[1,1,4]{2,1,0:T(1,128)} %param.24) | copy-start | bytes 52

commit v3 on v0

v3 whole, which is shorter than its diff:
```python
import jax
import jax.numpy as jnp
from jax import lax
from jax.experimental import pallas as pl
from jax.experimental.pallas import tpu as pltpu
from jax.sharding import PartitionSpec as P

HEADS = 8
BLOCK = 128
CH = 64
GROUP = 16
NX, NY, NZ = 4, 4, 4
PER_DEV = 3
PIECES = 2 * PER_DEV
HALF = PIECES // 2
SRC_BLOCKS = NX * NY * PER_DEV
N_COL = 2 * NZ
F32 = jnp.float32
BF16 = jnp.bfloat16
NT = (((1,), (1,)), ((), ()))
TN = (((0,), (0,)), ((), ()))
MESH = pl.DeviceIdType.MESH


def iota(shape, dim):
    return lax.broadcasted_iota(jnp.int32, shape, dim)


def dot(a, b, dims=(((1,), (0,)), ((), ()))):
    return lax.dot_general(a, b, dims, preferred_element_type=F32)


def where01(mask):
    return jnp.where(mask, 1.0, 0.0).astype(BF16)


def place():
    row, col = lax.axis_index("row"), lax.axis_index("col")
    x, y, z, core = row // NY, row % NY, col // 2, col % 2

    def on_x(k):
        return (lax.rem(x + k, NX) * NY + y, col)

    def on_y(k):
        return (x * NY + lax.rem(y + k, NY), col)

    def on_z(k):
        return (row, lax.rem(z + k, NZ) * 2 + core)

    return x, y, z, core, on_x, on_y, on_z, (row, z * 2 + 1 - core)


def remote(src, dst, send_sem, recv_sem, peer):
    return pltpu.make_async_remote_copy(
        src_ref=src, dst_ref=dst, send_sem=send_sem, recv_sem=recv_sem, device_id=peer, device_id_type=MESH
    )


def build_maps(wb_ref, wg_ref, wo_ref, mix_map, out_map):
    rows, cols = 2 * HEADS * GROUP, CH * GROUP
    pick = iota((rows, HEADS), 0) >> 4
    head = iota((rows, HEADS), 1)
    picked = dot(where01(pick == head), wb_ref[...]) + dot(where01(pick == head + HEADS), wg_ref[...])
    spread = where01(iota((CH, cols), 0) == iota((CH, cols), 1) >> 4)
    full = dot(picked.astype(BF16), spread)
    same = (iota((rows, cols), 0) & 15) == (iota((rows, cols), 1) & 15)
    mix_map[...] = jnp.where(same, full, 0.0).astype(BF16)
    narrow = HEADS * GROUP
    w_out = wo_ref[...]
    high = w_out.astype(BF16)
    low = (w_out - high.astype(F32)).astype(BF16)
    pick = where01(iota((cols, CH), 0) >> 4 == iota((cols, CH), 1))
    spread = where01(iota((HEADS, narrow), 0) == iota((HEADS, narrow), 1) >> 4)
    same = (iota((cols, narrow), 0) & 15) == (iota((cols, narrow), 1) & 15)
    for part, w in enumerate((high, low)):
        full = dot(dot(pick, w, NT).astype(BF16), spread)
        out_map[:, part * narrow : (part + 1) * narrow] = jnp.where(same, full, 0.0).astype(BF16)


def group_rows(g, side):
    return pl.ds(pl.multiple_of(g * (2 * GROUP) + side * GROUP, GROUP), GROUP)


def both(f):
    return jnp.concatenate([f(0), f(1)], axis=1)


def edge_terms(slot, edge_s, mix_map, bias_s, gate_s):
    def pair(g, _):
        edge2 = both(lambda side: edge_s[slot, :, group_rows(g, side), :].reshape(CH * GROUP, BLOCK))
        mix = dot(mix_map[...], edge2)
        bias, gate = mix[: HEADS * GROUP], mix[HEADS * GROUP :]
        gate = 1.0 / (1.0 + jnp.exp(-gate))
        for side in range(2):
            part = slice(side * BLOCK, (side + 1) * BLOCK)
            bias_s[slot, :, group_rows(g, side), :] = bias[:, part].reshape(HEADS, GROUP, BLOCK)
            gate_s[slot, :, group_rows(g, side), :] = gate[:, part].reshape(HEADS, GROUP, BLOCK)
        return 0

    lax.fori_loop(0, BLOCK // (2 * GROUP), pair, 0)


def project(x, w_s, y_s):
    width = w_s.shape[0]
    for n in range(0, width, 256):
        y_s[:, :, n : n + 256] = dot(x, w_s[:, n : n + 256]).astype(BF16).reshape(-1, BLOCK, 256)


def attend(slot, live, q_s, k_s, v_s, bias_s, gate_s, score_s, weight_s, expo_s, numer_s, denom_s):
    width = q_s.shape[-1]
    head_dim = width // HEADS
    for h in range(HEADS):
        lo, hi = h * head_dim, (h + 1) * head_dim
        a, b = lo // 128 * 128, -(-hi // 128) * 128
        lane = iota((BLOCK, b - a), 1) + a
        q = q_s[slot, :, a:b]
        q = jnp.where((lane >= lo) & (lane < hi), q, jnp.zeros_like(q))
        raw = dot(q, k_s[slot, :, a:b], NT)
        score = jnp.clip(raw * (1.0 / head_dim**0.5), -5.0, 5.0) + bias_s[slot, h]
        expo = jnp.exp(score)
        score_s[slot, h] = score.astype(BF16)
        weight_s[h] = (expo * gate_s[slot, h]).astype(BF16)
        expo_s[:, h * BLOCK : (h + 1) * BLOCK] = expo.astype(BF16)
    for m in range(width // 128):
        heads = range(m * 128 // head_dim, (m * 128 + 127) // head_dim + 1)
        v = v_s[slot, :, m * 128 : (m + 1) * 128]
        lane = iota((BLOCK, 128), 1) + m * 128
        weights = jnp.concatenate([weight_s[h] for h in heads], axis=1)
        values = jnp.concatenate(
            [
                jnp.where((lane >= h * head_dim) & (lane < (h + 1) * head_dim), v, jnp.zeros_like(v))
                for h in heads
            ],
            axis=0,
        )
        numer = dot(weights, values)
        numer = jnp.where(live, numer, jnp.zeros_like(numer)).astype(BF16)
        piece = BLOCK // 2
        numer_s[2 * slot, :, m * 128 : (m + 1) * 128] = numer[:piece]
        numer_s[2 * slot + 1, :, m * 128 : (m + 1) * 128] = numer[piece:]
    ones = where01(iota((HEADS, HEADS * BLOCK), 0) == iota((HEADS, HEADS * BLOCK), 1) >> 7)
    denom = dot(ones, expo_s[...], NT)
    denom_s[slot] = jnp.where(live, denom, jnp.zeros_like(denom))


def edge_output(slot, live, gain_ref, out_map, edge_s, score_s, mixed_s):
    factor = jnp.where(live, 1.0, 0.0)

    def pair(g, _):
        score = both(lambda side: score_s[slot, :, group_rows(g, side), :].reshape(HEADS * GROUP, BLOCK))
        mixed_s[...] = dot(out_map[...], jnp.concatenate([score, score], axis=0))
        for side in range(2):
            part = slice(side * BLOCK, (side + 1) * BLOCK)
            rows = group_rows(g, side)
            total = jnp.zeros((GROUP, BLOCK), F32)
            for c in range(CH):
                m = mixed_s[c * GROUP : (c + 1) * GROUP, part] + edge_s[slot, c, rows, :].astype(F32)
                mixed_s[c * GROUP : (c + 1) * GROUP, part] = m
                total += m * m
            scale = lax.rsqrt(total * (1.0 / CH) + 1e-5) * factor
            for c in range(CH):
                m = mixed_s[c * GROUP : (c + 1) * GROUP, part]
                edge_s[slot, c, rows, :] = (m * (scale * gain_ref[c])).astype(BF16)
        return 0

    lax.fori_loop(0, BLOCK // (2 * GROUP), pair, 0)


def layer_kernel(
    tile_ref,
    count_ref,
    gain_edge_ref,
    nodes_ref,
    wb_ref,
    wg_ref,
    wo_ref,
    gain_node_ref,
    wq_hbm,
    wk_hbm,
    wv_hbm,
    wout_hbm,
    edges_hbm,
    nodes_out,
    edges_out,
    pool_y,
    pool_x,
    pool_z,
    fill_send,
    fill_recv,
    core_send,
    core_recv,
    meta_own,
    meta_vmem,
    meta,
    ring_send_sem,
    ring_recv_sem,
    fill_send_sem,
    fill_recv_sem,
    meta_send_sem,
    meta_recv_sem,
    core_sem,
    local_sem,
    edge_s,
    w_s,
    src_s,
    dest_s,
    q_s,
    k_s,
    v_s,
    mix_map,
    out_map,
    bias_s,
    gate_s,
    score_s,
    weight_s,
    expo_s,
    mixed_s,
    numer_s,
    denom_s,
    edge_sem,
    w_sem,
    sib_numer,
    send,
    recv,
    den_send,
    den_recv,
    sib_send_sem,
    sib_recv_sem,
    send_sem,
    recv_sem,
    den_send_sem,
    den_recv_sem,
):
    x, y, z, core, on_x, on_y, on_z, sibling = place()
    row, col = lax.axis_index("row"), lax.axis_index("col")
    width = nodes_ref.shape[-1]
    head_dim = width // HEADS
    half = width // 2
    slots = edge_s.shape[0]
    piece = BLOCK // 2

    w_copies = []
    for i, w_hbm in enumerate((wq_hbm, wk_hbm, wv_hbm, wout_hbm)):
        w_copies.append(pltpu.make_async_copy(w_hbm, w_s.at[i], w_sem.at[i]))
    edge_copies = []
    for s in range(slots):
        edge_copies.append(pltpu.make_async_copy(edges_hbm.at[s], edge_s.at[s], edge_sem.at[s]))
        edge_copies[s].start()
    for copy in w_copies:
        copy.start()

    others = [(row, lax.rem(col + k, N_COL)) for k in range(1, N_COL)]
    peers = [on_x(1), on_x(3), on_x(2), on_y(1), on_y(3), on_y(2)] + others
    barrier = pltpu.get_barrier_semaphore()
    for peer in peers:
        pl.semaphore_signal(barrier, inc=1, device_id=peer, device_id_type=MESH)
    lane = iota(meta_own.shape, 1)
    words = jnp.zeros(meta_own.shape, jnp.int32)
    for s in range(slots):
        words = jnp.where(lane == s, tile_ref[s] % SRC_BLOCKS, words)
        words = jnp.where(lane == slots + s, tile_ref[s] // SRC_BLOCKS, words)
    meta_own[...] = words
    pl.semaphore_wait(barrier, len(peers))

    meta_copies = []
    for peer, there in (
        (on_x(3), 0),
        (on_x(1), 1),
        (on_x(2), 2),
        (on_y(3), 3),
        (on_y(1), 4),
        (on_y(2), 5),
        (sibling, 6),
    ):
        copy = remote(meta_own, meta_vmem.at[there], meta_send_sem.at[there], meta_recv_sem.at[there], peer)
        copy.start()
        meta_copies.append(copy)

    rings = [(pool_y, y, on_y, 0, half), (pool_x, x, on_x, half, width), (pool_z, z, on_z, 0, width)]
    low, high = pl.ds(0, HALF), pl.ds(HALF, HALF)
    ring_copies = []
    for r, (pool, pos, on, a, b) in enumerate(rings):
        copies = {}
        for step in range(2):
            for way in range(2):
                part = step if way == 0 else 1 - step
                copies[way, step] = remote(
                    nodes_ref.at[(low, high)[part], :, a:b],
                    pool.at[pl.ds(pos * PIECES + part * HALF, HALF)],
                    ring_send_sem.at[r, way, step],
                    ring_recv_sem.at[r, way, step],
                    on(1 + 2 * way),
                )
        ring_copies.append(copies)
    for step in range(2):
        for r in range(3):
            for way in range(2):
                ring_copies[r][way, step].start()
    for pool, pos, on, a, b in rings:
        pool[pl.ds(pos * PIECES, PIECES)] = nodes_ref[:, :, a:b]

    build_maps(wb_ref, wg_ref, wo_ref, mix_map, out_map)

    def forward(r):
        pool, pos, on, a, b = rings[r]
        for way in range(2):
            owner = lax.rem(pos + 3 - 2 * way, 4)
            ring_copies[r][way, 0].wait_recv()
            here = pool.at[pl.ds(owner * PIECES + way * HALF, HALF)]
            ring_copies[r][way, 2] = remote(
                here, here, ring_send_sem.at[r, way, 2], ring_recv_sem.at[r, way, 2], on(1 + 2 * way)
            )
            ring_copies[r][way, 2].start()

    def terms(s):
        edge_copies[s].wait()
        edge_terms(s, edge_s, mix_map, bias_s, gate_s)

    forward(0)
    forward(1)
    terms(0)
    forward(2)
    for copy in meta_copies:
        copy.wait_recv()
    to_smem = pltpu.make_async_copy(meta_vmem, meta, local_sem)
    to_smem.start()
    terms(1)
    to_smem.wait()

    def source(who, s):
        block = tile_ref[s] % SRC_BLOCKS if who is None else meta[who, 0, s]
        t, o = block // PER_DEV, block % PER_DEV
        return t // NY, t % NY, o

    def along_x(who, s):
        bx, by, o = source(who, s)
        return bx, by * PER_DEV + o

    def along_y(who, s):
        bx, by, o = source(who, s)
        return by, bx * PER_DEV + o

    def load(pool, block):
        return pool[pl.ds(block * 2, 2)]

    fills = [(pool_y, x, on_x, along_x, (0, 1, 2)), (pool_x, y, on_y, along_y, (3, 4, 5))]
    fill_copies = []

    def send_fill(f, way, part, peer):
        copy = remote(
            fill_send.at[f, way, part],
            fill_recv.at[f, way, part],
            fill_send_sem.at[f, way, part],
            fill_recv_sem.at[f, way, part],
            peer,
        )
        copy.start()
        return copy

    for f, (pool, pos, on, along, (plus, minus, far)) in enumerate(fills):
        for way in range(2):
            for step in (1, 2):
                ring_copies[f][way, step].wait_recv()
        copies = {}
        for part, who_of in ((0, (far, far)), (1, (plus, minus))):
            for way in range(2):
                first = 2 * (way if part == 0 else 1 - way)
                for k in range(2):
                    fill_send[f, way, part, k] = load(pool, along(who_of[way], first + k)[1])
                copies[way, part] = send_fill(f, way, part, on(1 + 2 * way))
        fill_copies.append(copies)
    terms(2)
    for f, (pool, pos, on, along, (plus, minus, far)) in enumerate(fills):
        copies = fill_copies[f]
        for way, who in ((0, plus), (1, minus)):
            copies[way, 0].wait_recv()
            for k in range(2):
                at, block = along(who, 2 * way + k)
                fill_send[f, way, 2, k] = jnp.where(at == pos, load(pool, block), fill_recv[f, way, 0, k])
            copies[way, 2] = send_fill(f, way, 2, on(1 + 2 * way))
    terms(3)
    for copy in w_copies:
        copy.wait()

    for way in range(2):
        for step in (1, 2):
            ring_copies[2][way, step].wait_recv()

    def dest(who, s):
        block = tile_ref[s] // SRC_BLOCKS if who is None else meta[who, 0, slots + s]
        owner, o = block // PER_DEV, block % PER_DEV
        return owner % 2, (owner // 2) * PER_DEV + o

    for s in range(slots):
        core_send[s] = load(pool_z, dest(6, s)[1])
    core_copy = remote(core_send, core_recv, core_sem.at[0], core_sem.at[1], sibling)
    core_copy.start()
    core_copy.wait_recv()
    for s in range(slots):
        at, block = dest(None, s)
        dest_s[s] = jnp.where(at == core, load(pool_z, block), core_recv[s])
    project(dest_s[...].reshape(-1, width), w_s.at[0], q_s)

    for f, (pool, pos, on, along, (plus, minus, far)) in enumerate(fills):
        copies = fill_copies[f]
        for way in range(2):
            for part in (1, 2):
                copies[way, part].wait_recv()
        for s in range(slots):
            at, block = along(None, s)
            own = load(pool, block)
            k = s % 2
            if s < 2:
                near, other = fill_recv[f, 1, 1, k], fill_recv[f, 0, 2, k]
                is_near = at == lax.rem(pos + 1, 4)
            else:
                near, other = fill_recv[f, 0, 1, k], fill_recv[f, 1, 2, k]
                is_near = at == lax.rem(pos + 3, 4)
            src_s[s, :, :, f * half : (f + 1) * half] = jnp.where(
                at == pos, own, jnp.where(is_near, near, other)
            )
    project(src_s[...].reshape(-1, width), w_s.at[1], k_s)
    project(src_s[...].reshape(-1, width), w_s.at[2], v_s)

    lives = [s < count_ref[0] for s in range(slots)]
    sib_copies = []
    for s in range(slots):
        attend(
            s, lives[s], q_s, k_s, v_s, bias_s, gate_s, score_s, weight_s, expo_s, numer_s, denom_s
        )
        here = pl.ds(2 * s, 2)
        copy = remote(numer_s.at[here], sib_numer.at[here], sib_send_sem.at[s], sib_recv_sem.at[s], sibling)
        copy.start()
        sib_copies.append(copy)

    mine = [tile_ref[s] // SRC_BLOCKS for s in range(slots)]
    theirs = [meta[6, 0, slots + s] for s in range(slots)]

    def find(ids, a):
        index, found = jnp.int32(0), jnp.int32(0)
        for s in range(slots):
            index = jnp.where(ids[s] == a, s, index)
            found = jnp.where(ids[s] == a, 1, found)
        return index, found

    def denom_of(owner, o):
        index, found = find(mine, owner * PER_DEV + o)
        d = denom_s[index]
        return jnp.where(found > 0, d, jnp.zeros_like(d))

    for copy in sib_copies:
        copy.wait_recv()

    def chunk(at, p):
        a = (at * 2 + core) * PER_DEV + p // 2
        i, f = find(mine, a)
        j, g = find(theirs, a)
        u = numer_s[i * 2 + p % 2].astype(F32)
        v = sib_numer[j * 2 + p % 2].astype(F32)
        return jnp.where(f > 0, u, jnp.zeros_like(u)) + jnp.where(g > 0, v, jnp.zeros_like(v))

    copies = {}

    def start(way, part):
        copies[way, part] = remote(
            send.at[way, part],
            recv.at[way, part],
            send_sem.at[way, part],
            recv_sem.at[way, part],
            on_z(1 + 2 * way),
        )
        copies[way, part].start()

    for part in range(2):
        for way in range(2):
            at = lax.rem(z + (2 if part == 0 else 1 + 2 * way), NZ)
            first = HALF * (way if part == 0 else 1 - way)
            for k in range(HALF):
                send[way, part, k] = chunk(at, first + k).astype(BF16)
            start(way, part)
    den_copies = []
    for k in range(1, N_COL):
        for o in range(PER_DEV):
            den_send[k, o] = denom_of(lax.rem(col + k, N_COL), o)
        copy = remote(den_send.at[k], den_recv.at[k], den_send_sem.at[k], den_recv_sem.at[k], others[k - 1])
        copy.start()
        den_copies.append(copy)

    out_copies = []

    def emit(s):
        edge_output(s, lives[s], gain_edge_ref, out_map, edge_s, score_s, mixed_s)
        copy = pltpu.make_async_copy(edge_s.at[s], edges_out.at[s], edge_sem.at[s])
        copy.start()
        out_copies.append(copy)

    emit(0)
    emit(1)
    emit(2)
    for way in range(2):
        at = lax.rem(z + 1 + 2 * way, NZ)
        copies[way, 0].wait_recv()
        for k in range(HALF):
            send[way, 2, k] = (chunk(at, HALF * way + k) + recv[way, 0, k].astype(F32)).astype(BF16)
        start(way, 2)
    emit(3)
    for copy in den_copies:
        copy.wait_recv()
    heads = iota((2 * HEADS, width), 0) & 7
    lanes = iota((2 * HEADS, width), 1)
    expand = where01((lanes >= heads * head_dim) & (lanes < (heads + 1) * head_dim))
    scales = []
    for o in range(PER_DEV):
        d = denom_of(col, o)
        for k in range(1, N_COL):
            d += den_recv[k, o]
        inverse = jnp.where(d > 0.0, 1.0 / jnp.where(d > 0.0, d, 1.0), 0.0)
        upper = inverse.astype(BF16).astype(F32)
        scales.append(dot(jnp.concatenate([upper, inverse - upper], axis=0).astype(BF16), expand, TN))
    for part in (1, 2):
        for way in range(2):
            copies[way, part].wait_recv()
    for o in range(PER_DEV):
        parts = []
        for p in (2 * o, 2 * o + 1):
            k = p % HALF
            left, right = (2, 1) if p < HALF else (1, 2)
            parts.append(chunk(z, p) + recv[0, left, k].astype(F32) + recv[1, right, k].astype(F32))
        numer = jnp.concatenate(parts, axis=0)
        attended = (numer * scales[o]).astype(BF16)
        base = nodes_ref[2 * o : 2 * o + 2].reshape(BLOCK, width).astype(F32)
        mixed = base + dot(attended, w_s[3])
        mean = jnp.mean(mixed * mixed, axis=1, keepdims=True)
        nodes_out[o * BLOCK : (o + 1) * BLOCK] = (
            mixed * lax.rsqrt(mean + 1e-05) * gain_node_ref[...]
        ).astype(BF16)

    for copy in out_copies:
        copy.wait()
    core_copy.wait_send()
    for copy in meta_copies + sib_copies + den_copies:
        copy.wait_send()
    for group in ring_copies + fill_copies + [copies]:
        for copy in group.values():
            copy.wait_send()


def on_device(
    nodes,
    w_query,
    w_key,
    w_value,
    w_out,
    w_edge_gate,
    w_edge_bias,
    w_edge_out,
    gain_node,
    gain_edge,
    edges,
    tile_list,
    tile_count,
):
    rows, width = nodes.shape
    slots = edges.shape[2]
    piece = rows // PIECES
    half = width // 2
    vm = pl.BlockSpec(memory_space=pltpu.VMEM)
    sm = pl.BlockSpec(memory_space=pltpu.SMEM)
    hbm = pl.BlockSpec(memory_space=pl.ANY)
    dma = pltpu.SemaphoreType.DMA
    v = pltpu.VMEM
    nodes_out, edges_out = pl.pallas_call(
        layer_kernel,
        in_specs=[sm, sm, sm] + [vm] * 5 + [hbm] * 5,
        out_specs=[vm, hbm],
        out_shape=[
            jax.ShapeDtypeStruct((rows, width), BF16),
            jax.ShapeDtypeStruct((slots, CH, BLOCK, BLOCK), BF16),
        ],
        scratch_shapes=[
            v((4 * PIECES, piece, half), BF16),
            v((4 * PIECES, piece, half), BF16),
            v((4 * PIECES, piece, width), BF16),
            v((2, 2, 3, 2, 2, piece, half), BF16),
            v((2, 2, 3, 2, 2, piece, half), BF16),
            v((slots, 2, piece, width), BF16),
            v((slots, 2, piece, width), BF16),
            v((8, 128), jnp.int32),
            v((7, 8, 128), jnp.int32),
            pltpu.SMEM((7, 8, 128), jnp.int32),
            dma((3, 2, 3)),
            dma((3, 2, 3)),
            dma((2, 2, 3)),
            dma((2, 2, 3)),
            dma((7,)),
            dma((7,)),
            dma((2,)),
            dma,
            v((slots, CH, BLOCK, BLOCK), BF16),
            v((4, width, width), BF16),
            v((slots, 2, piece, width), BF16),
            v((slots, 2, piece, width), BF16),
            v((slots, BLOCK, width), BF16),
            v((slots, BLOCK, width), BF16),
            v((slots, BLOCK, width), BF16),
            v((2 * HEADS * GROUP, CH * GROUP), BF16),
            v((CH * GROUP, 2 * HEADS * GROUP), BF16),
            v((slots, HEADS, BLOCK, BLOCK), F32),
            v((slots, HEADS, BLOCK, BLOCK), F32),
            v((slots, HEADS, BLOCK, BLOCK), BF16),
            v((HEADS, BLOCK, BLOCK), BF16),
            v((BLOCK, HEADS * BLOCK), BF16),
            v((CH * GROUP, 2 * BLOCK), F32),
            v((2 * slots, piece, width), BF16),
            v((slots, HEADS, BLOCK), F32),
            dma((slots,)),
            dma((4,)),
            v((2 * slots, piece, width), BF16),
            v((2, 3, HALF, piece, width), BF16),
            v((2, 3, HALF, piece, width), BF16),
            v((N_COL, PER_DEV, HEADS, BLOCK), F32),
            v((N_COL, PER_DEV, HEADS, BLOCK), F32),
            dma((slots,)),
            dma((slots,)),
            dma((2, 3)),
            dma((2, 3)),
            dma((N_COL,)),
            dma((N_COL,)),
        ],
        compiler_params=pltpu.CompilerParams(
            collective_id=0, has_side_effects=True, vmem_limit_bytes=60 * 1024 * 1024
        ),
        name="layer",
    )(
        tile_list.reshape(-1),
        tile_count.reshape(1),
        gain_edge,
        nodes.reshape(PIECES, piece, width),
        w_edge_bias.T,
        w_edge_gate.T,
        w_edge_out,
        gain_node.reshape(1, width),
        w_query,
        w_key,
        w_value,
        w_out,
        edges.reshape(slots, CH, BLOCK, BLOCK),
    )
    return (nodes_out, edges_out.reshape(edges.shape))


def solution(mesh):
    return jax.shard_map(
        on_device,
        mesh=mesh,
        in_specs=(
            P(("row", "col"), None),
            *[P()] * 9,
            P("row", "col", None, None, None, None),
            P("row", "col", None),
            P("row", "col"),
        ),
        out_specs=(P(("row", "col"), None), P("row", "col", None, None, None, None)),
        check_vma=False,
    )
```

time: 323 us -> 80.4 us (0.25); the launches traced: 317 us -> 80.2 us
  waiting for transfers between devices: 112 us -> 0 us
  Pallas kernels: 0 us -> 65.2 us
  matrix products: 58.3 us -> 0 us
  local copies, waits for them, and re-layouts: 62.8 us -> 13.7 us
  other arithmetic: 36.7 us -> 0 us
  blocking collectives: 23.5 us -> 0 us
  between operations: 23.2 us -> 1.29 us
    all_gather x2 -> x0, waiting for transfers between devices: 112 us -> none  [the longest x1 112 us: on_device(): sources = lax.all_gather(pair_own, 'row', axis=0, tiled=True)]
    pallas_call x0 -> x1, Pallas kernels: none -> 65.2 us  [on_device(): pl.pallas_call(layer_kernel, in_specs=[sm, sm, sm] + [vm] * 5 + [hbm] * 5...]
    dot_general x19 -> x0, matrix products: 58.3 us -> none  [the longest x4 30.2 us: tile_step(): jnp.einsum('hij,hc->cij', score, w_edge_out, precision=lax.Precision.HIGH...]
    another operation x1 -> x0, other arithmetic: 23.5 us -> none  [on_device(): edges_out = jnp.stack(new_edges, axis=0)[None, None]]
    psum x1 -> x0, blocking collectives: 23.5 us -> none  [on_device(): lax.psum(denom.astype(jnp.bfloat16), 'col').astype(jnp.float32)]
    unnamed x57 -> x2, local copies, waits for them, and re-layouts: 31.5 us -> 12.4 us
    slice x7 -> x0, local copies, waits for them, and re-layouts: 13.7 us -> none  [the longest x1 6.19 us: on_device(): edges[0, 0, slot]]
    dynamic_slice x5 -> x0, local copies, waits for them, and re-layouts: 8.23 us -> none  [on_device(): query_block = lax.dynamic_slice_in_dim(queries, dest_start, BLOCK, 0)]
  transfers between devices with their start and end apart: 3 -> 0, of which waited for: 1 -> 0; matrix products, arithmetic and copies ran while one was open for 38% -> 0% of each run, Pallas kernels for 0% -> 0%
where the time goes in v3:
time: 80.4 us; the launch traced here: 80.2 us
  Pallas kernels  65.2 us (81%)
  local copies, waits for them, and re-layouts  13.7 us (17%)
  between operations  1.29 us (2%)
    pallas_call x1, Pallas kernels, on_device(): pl.pallas_call(layer_kernel, in_specs=[sm, sm, sm] + [vm] * 5 + [hbm] * 5...  65.2 us
    unnamed x2, local copies, waits for them, and re-layouts  12.4 us

profile of v3, /device:TPU:1, one launch (start us, length us, event | category | flops | bytes accessed | tf_op | source)
XLA Modules:
  0.0 80.2 jit_solution(999217281367256514)
XLA Ops:
  1.3 1.3 %reshape.25.gain_node_ref = f32[1,768]{1,0:T(1,128)} reshape(f32[768]{0:T(1024)} %param.21) | data formatting | bytes 6144 | tf_op jit(solution)/shard_map/reshape | solution.py:642
  2.5 65.2 %layer.1 = (bf16[384,768]{1,0:T(8,128)(2,1)}, bf16[4,64,128,128]{3,2,1,0:T(8,128)(2,1)}) custom-call(s32[4]{0:T(128)} %bitcast.13, s32[1]{0:T(128)} %bitcast.7.count_ref, f32[64]{0:T(128)} %gain_edge_ref.1, bf16[6,64,768]{2,1,0:T(8,128)(2,1)} %bitcast.10, bf16[8,64]{1,0:T(8,128)(2,1)} %bitcast.11, bf16[8,64]{1,0:T(8,128)(2,1)} %bitcast.12, f32[8,64]{1,0:T(8,128)} %wo_ref.1, ...), custom_call_target="tpu_custom_call" | custom-call | tf_op jit(solution)/shard_map/layer/pallas_call | solution.py:572
  67.8 1.9 %copy.18 = bf16[384,768]{1,0:T(8,128)(2,1)} copy(bf16[384,768]{1,0:T(8,128)(2,1)} %get-tuple-element.8) | data formatting | bytes 1179648
  69.7 10.5 %copy.19 = bf16[1,1,4,64,128,128]{5,4,3,2,1,0:T(8,128)(2,1)} copy(bf16[1,1,4,64,128,128]{5,4,3,2,1,0:T(8,128)(2,1)} %bitcast.9) | data formatting | bytes 16777216

commit v4 on v3

--- a/solution.py
+++ b/solution.py
@@ -181,7 +181,7 @@
     wout_hbm,
     edges_hbm,
     nodes_out,
-    edges_out,
+    edge_s,
     pool_y,
     pool_x,
     pool_z,
@@ -200,7 +200,6 @@
     meta_recv_sem,
     core_sem,
     local_sem,
-    edge_s,
     w_s,
     src_s,
     dest_s,
@@ -486,13 +485,8 @@
         copy.start()
         den_copies.append(copy)
 
-    out_copies = []
-
     def emit(s):
         edge_output(s, lives[s], gain_edge_ref, out_map, edge_s, score_s, mixed_s)
-        copy = pltpu.make_async_copy(edge_s.at[s], edges_out.at[s], edge_sem.at[s])
-        copy.start()
-        out_copies.append(copy)
 
     emit(0)
     emit(1)
@@ -532,11 +526,9 @@
         mixed = base + dot(attended, w_s[3])
         mean = jnp.mean(mixed * mixed, axis=1, keepdims=True)
         nodes_out[o * BLOCK : (o + 1) * BLOCK] = (
-            mixed * lax.rsqrt(mean + 1e-05) * gain_node_ref[...]
+            mixed * lax.rsqrt(mean + 1e-05) * gain_node_ref[...][None]
         ).astype(BF16)
 
-    for copy in out_copies:
-        copy.wait()
     core_copy.wait_send()
     for copy in meta_copies + sib_copies + den_copies:
         copy.wait_send()
@@ -572,11 +564,8 @@
     nodes_out, edges_out = pl.pallas_call(
         layer_kernel,
         in_specs=[sm, sm, sm] + [vm] * 5 + [hbm] * 5,
-        out_specs=[vm, hbm],
-        out_shape=[
-            jax.ShapeDtypeStruct((rows, width), BF16),
-            jax.ShapeDtypeStruct((slots, CH, BLOCK, BLOCK), BF16),
-        ],
+        out_specs=[vm, vm],
+        out_shape=[v((rows, width), BF16), v((slots, CH, BLOCK, BLOCK), BF16)],
         scratch_shapes=[
             v((4 * PIECES, piece, half), BF16),
             v((4 * PIECES, piece, half), BF16),
@@ -596,7 +585,6 @@
             dma((7,)),
             dma((2,)),
             dma,
-            v((slots, CH, BLOCK, BLOCK), BF16),
             v((4, width, width), BF16),
             v((slots, 2, piece, width), BF16),
             v((slots, 2, piece, width), BF16),
@@ -628,7 +616,7 @@
             dma((N_COL,)),
         ],
         compiler_params=pltpu.CompilerParams(
-            collective_id=0, has_side_effects=True, vmem_limit_bytes=60 * 1024 * 1024
+            collective_id=0, has_side_effects=True, vmem_limit_bytes=50 * 1024 * 1024
         ),
         name="layer",
     )(
@@ -639,13 +627,14 @@
         w_edge_bias.T,
         w_edge_gate.T,
         w_edge_out,
-        gain_node.reshape(1, width),
+        gain_node,
         w_query,
         w_key,
         w_value,
         w_out,
         edges.reshape(slots, CH, BLOCK, BLOCK),
     )
+
     return (nodes_out, edges_out.reshape(edges.shape))
 
 

time: 80.4 us -> 70 us (0.87)
  local copies, waits for them, and re-layouts: 13.7 us -> 4.21 us
    unnamed x2, local copies, waits for them, and re-layouts: 12.4 us -> 4.21 us
    reshape x1 -> x0, local copies, waits for them, and re-layouts: 1.27 us -> none  [on_device(): gain_node.reshape(1, width)]
    pallas_call x1, Pallas kernels: 65.2 us -> 64.4 us  [on_device(): pl.pallas_call(layer_kernel, in_specs=[sm, sm, sm] + [vm] * 5 + [hbm] * 5...]
where the time goes in v4:
time: 70 us; the launch traced here: 69.9 us
  Pallas kernels  64.4 us (92%)
  local copies, waits for them, and re-layouts  4.21 us (6%)
  between operations  1.29 us (2%)
    pallas_call x1, Pallas kernels, on_device(): pl.pallas_call(layer_kernel, in_specs=[sm, sm, sm] + [vm] * 5 + [hbm] * 5...  64.4 us
    unnamed x2, local copies, waits for them, and re-layouts  4.21 us

profile of v4, /device:TPU:1, one launch (start us, length us, event | category | flops | bytes accessed | tf_op | source)
XLA Modules:
  0.0 69.9 jit_solution(10599979361243665324)
XLA Ops:
  1.3 64.4 %layer.1 = (bf16[384,768]{1,0:T(8,128)(2,1)S(1)}, bf16[4,64,128,128]{3,2,1,0:T(8,128)(2,1)S(1)}) custom-call(s32[4]{0:T(128)} %bitcast.13, s32[1]{0:T(128)} %bitcast.7.count_ref, f32[64]{0:T(128)} %gain_edge_ref.1, bf16[6,64,768]{2,1,0:T(8,128)(2,1)} %bitcast.10, bf16[8,64]{1,0:T(8,128)(2,1)} %bitcast.11, bf16[8,64]{1,0:T(8,128)(2,1)} %bitcast.12, ...), custom_call_target="tpu_custom_call" | custom-call | tf_op jit(solution)/shard_map/layer/pallas_call | solution.py:564
  65.7 0.8 %copy.17 = bf16[384,768]{1,0:T(8,128)(2,1)} copy(bf16[384,768]{1,0:T(8,128)(2,1)S(1)} %get-tuple-element.6) | data formatting | bytes 1179648
  66.5 3.4 %copy.18 = bf16[1,1,4,64,128,128]{5,4,3,2,1,0:T(8,128)(2,1)} copy(bf16[1,1,4,64,128,128]{5,4,3,2,1,0:T(8,128)(2,1)S(1)} %bitcast.8) | data formatting | bytes 16777216

commit v5 on v4

v5 whole, which is shorter than its diff:
```python
import jax
import jax.numpy as jnp
from jax import lax
from jax.experimental import pallas as pl
from jax.experimental.pallas import tpu as pltpu
from jax.sharding import PartitionSpec as P

HEADS = 8
BLOCK = 128
CH = 64
GROUP = 16
NX, NY, NZ = 4, 4, 4
PER_DEV = 3
PIECES = 2 * PER_DEV
HALF = PIECES // 2
SRC_BLOCKS = NX * NY * PER_DEV
N_COL = 2 * NZ
F32 = jnp.float32
BF16 = jnp.bfloat16
NT = (((1,), (1,)), ((), ()))
TN = (((0,), (0,)), ((), ()))
MESH = pl.DeviceIdType.MESH


def iota(shape, dim):
    return lax.broadcasted_iota(jnp.int32, shape, dim)


def dot(a, b, dims=(((1,), (0,)), ((), ()))):
    return lax.dot_general(a, b, dims, preferred_element_type=F32)


def where01(mask):
    return jnp.where(mask, 1.0, 0.0).astype(BF16)


def place():
    row, col = lax.axis_index("row"), lax.axis_index("col")
    x, y, z, core = row // NY, row % NY, col // 2, col % 2

    def on_x(k):
        return (lax.rem(x + k, NX) * NY + y, col)

    def on_y(k):
        return (x * NY + lax.rem(y + k, NY), col)

    def on_z(k):
        return (row, lax.rem(z + k, NZ) * 2 + core)

    return x, y, z, core, on_x, on_y, on_z, (row, z * 2 + 1 - core)


def remote(src, dst, send_sem, recv_sem, peer):
    return pltpu.make_async_remote_copy(
        src_ref=src, dst_ref=dst, send_sem=send_sem, recv_sem=recv_sem, device_id=peer, device_id_type=MESH
    )


def build_maps(wb_ref, wg_ref, wo_ref, mix_map, out_map):
    rows, cols = 2 * HEADS * GROUP, CH * GROUP
    pick = iota((rows, HEADS), 0) >> 4
    head = iota((rows, HEADS), 1)
    picked = dot(where01(pick == head), wb_ref[...]) + dot(where01(pick == head + HEADS), wg_ref[...])
    spread = where01(iota((CH, cols), 0) == iota((CH, cols), 1) >> 4)
    full = dot(picked.astype(BF16), spread)
    same = (iota((rows, cols), 0) & 15) == (iota((rows, cols), 1) & 15)
    mix_map[...] = jnp.where(same, full, 0.0).astype(BF16)
    narrow = HEADS * GROUP
    w_out = wo_ref[...]
    high = w_out.astype(BF16)
    low = (w_out - high.astype(F32)).astype(BF16)
    pick = where01(iota((cols, CH), 0) >> 4 == iota((cols, CH), 1))
    spread = where01(iota((HEADS, narrow), 0) == iota((HEADS, narrow), 1) >> 4)
    same = (iota((cols, narrow), 0) & 15) == (iota((cols, narrow), 1) & 15)
    for part, w in enumerate((high, low)):
        full = dot(dot(pick, w, NT).astype(BF16), spread)
        out_map[:, part * narrow : (part + 1) * narrow] = jnp.where(same, full, 0.0).astype(BF16)


def group_rows(g, side):
    return pl.ds(pl.multiple_of(g * (2 * GROUP) + side * GROUP, GROUP), GROUP)


def both(f):
    return jnp.concatenate([f(0), f(1)], axis=1)


def edge_terms(slot, edge_s, mix_map, bias_s, gate_s):
    def pair(g, _):
        edge2 = both(lambda side: edge_s[slot, :, group_rows(g, side), :].reshape(CH * GROUP, BLOCK))
        mix = dot(mix_map[...], edge2)
        bias, gate = mix[: HEADS * GROUP], mix[HEADS * GROUP :]
        gate = 1.0 / (1.0 + jnp.exp(-gate))
        for side in range(2):
            part = slice(side * BLOCK, (side + 1) * BLOCK)
            bias_s[slot, :, group_rows(g, side), :] = bias[:, part].reshape(HEADS, GROUP, BLOCK)
            gate_s[slot, :, group_rows(g, side), :] = gate[:, part].reshape(HEADS, GROUP, BLOCK)
        return 0

    lax.fori_loop(0, BLOCK // (2 * GROUP), pair, 0)


def project(x_s, batch, w_s, y_s):
    width = w_s.shape[0]
    slots = slice(2 * batch, 2 * batch + 2)
    x = jnp.concatenate([x_s[side, slots].reshape(2 * BLOCK, width // 2) for side in range(2)], axis=1)
    for n in range(0, width, 256):
        y_s[slots, :, n : n + 256] = dot(x, w_s[:, n : n + 256]).astype(BF16).reshape(2, BLOCK, 256)


def attend(slot, live, q_s, k_s, v_s, bias_s, gate_s, score_s, weight_s, expo_s, numer_s, denom_s):
    width = q_s.shape[-1]
    head_dim = width // HEADS
    for h in range(HEADS):
        lo, hi = h * head_dim, (h + 1) * head_dim
        a, b = lo // 128 * 128, -(-hi // 128) * 128
        lane = iota((BLOCK, b - a), 1) + a
        q = q_s[slot, :, a:b]
        q = jnp.where((lane >= lo) & (lane < hi), q, jnp.zeros_like(q))
        raw = dot(q, k_s[slot, :, a:b], NT)
        score = jnp.clip(raw * (1.0 / head_dim**0.5), -5.0, 5.0) + bias_s[slot, h]
        expo = jnp.exp(score)
        score_s[slot, h] = score.astype(BF16)
        weight_s[h] = (expo * gate_s[slot, h]).astype(BF16)
        expo_s[:, h * BLOCK : (h + 1) * BLOCK] = expo.astype(BF16)
    for m in range(width // 128):
        heads = range(m * 128 // head_dim, (m * 128 + 127) // head_dim + 1)
        v = v_s[slot, :, m * 128 : (m + 1) * 128]
        lane = iota((BLOCK, 128), 1) + m * 128
        weights = jnp.concatenate([weight_s[h] for h in heads], axis=1)
        values = jnp.concatenate(
            [
                jnp.where((lane >= h * head_dim) & (lane < (h + 1) * head_dim), v, jnp.zeros_like(v))
                for h in heads
            ],
            axis=0,
        )
        numer = dot(weights, values)
        numer = jnp.where(live, numer, jnp.zeros_like(numer)).astype(BF16)
        side, first = divmod(m * 128, width // 2)
        numer_s[side, 2 * slot : 2 * slot + 2, :, first : first + 128] = numer.reshape(2, BLOCK // 2, 128)
    ones = where01(iota((HEADS, HEADS * BLOCK), 0) == iota((HEADS, HEADS * BLOCK), 1) >> 7)
    denom = dot(ones, expo_s[...], NT)
    denom_s[slot] = jnp.where(live, denom, jnp.zeros_like(denom))


def edge_output(slot, live, gain_ref, out_map, edge_s, score_s, mixed_s):
    factor = jnp.where(live, 1.0, 0.0)

    def pair(g, _):
        score = both(lambda side: score_s[slot, :, group_rows(g, side), :].reshape(HEADS * GROUP, BLOCK))
        mixed_s[...] = dot(out_map[...], jnp.concatenate([score, score], axis=0))
        for side in range(2):
            part = slice(side * BLOCK, (side + 1) * BLOCK)
            rows = group_rows(g, side)
            total = jnp.zeros((GROUP, BLOCK), F32)
            for c in range(CH):
                m = mixed_s[c * GROUP : (c + 1) * GROUP, part] + edge_s[slot, c, rows, :].astype(F32)
                mixed_s[c * GROUP : (c + 1) * GROUP, part] = m
                total += m * m
            scale = lax.rsqrt(total * (1.0 / CH) + 1e-5) * factor
            for c in range(CH):
                m = mixed_s[c * GROUP : (c + 1) * GROUP, part]
                edge_s[slot, c, rows, :] = (m * (scale * gain_ref[c])).astype(BF16)
        return 0

    lax.fori_loop(0, BLOCK // (2 * GROUP), pair, 0)


def layer_kernel(
    tile_ref,
    count_ref,
    gain_edge_ref,
    nodes_ref,
    wb_ref,
    wg_ref,
    wo_ref,
    gain_node_ref,
    wq_hbm,
    wk_hbm,
    wv_hbm,
    wout_hbm,
    edges_hbm,
    nodes_out,
    edge_s,
    nodes_h,
    pool_y,
    pool_x,
    pool_z,
    fill_send,
    fill_recv,
    wish_send,
    wish_recv,
    core_send,
    meta_own,
    meta_vmem,
    meta,
    ring_send_sem,
    ring_recv_sem,
    pair_send_sem,
    pair_recv_sem,
    fill_send_sem,
    fill_recv_sem,
    wish_send_sem,
    wish_recv_sem,
    meta_send_sem,
    meta_recv_sem,
    core_send_sem,
    core_recv_sem,
    local_sem,
    w_s,
    src_s,
    dest_s,
    q_s,
    k_s,
    v_s,
    mix_map,
    out_map,
    bias_s,
    gate_s,
    score_s,
    weight_s,
    expo_s,
    mixed_s,
    numer_s,
    denom_s,
    edge_sem,
    w_sem,
    sib_numer,
    pair_numer,
    sum_send,
    sum_recv,
    last_send,
    last_s,
    den_send,
    den_recv,
    sib_send_sem,
    sib_recv_sem,
    first_send_sem,
    first_recv_sem,
    sum_send_sem,
    sum_recv_sem,
    last_sem,
    den_send_sem,
    den_recv_sem,
):
    x, y, z, core, on_x, on_y, on_z, sibling = place()
    row, col = lax.axis_index("row"), lax.axis_index("col")
    width = gain_node_ref.shape[0]
    head_dim = width // HEADS
    half = width // 2
    slots = edge_s.shape[0]
    batches = slots // 2
    other = 1 - core
    flip, mirror = z + 1 - 2 * (z % 2), NZ - 1 - z
    near_z = flip * other + mirror * core
    far_z = mirror * other + flip * core
    near, far_pair = (row, near_z * 2 + core), (row, far_z * 2 + core)
    sends = []

    def push(src, dst, send_sem, recv_sem, peer):
        copy = remote(src, dst, send_sem, recv_sem, peer)
        copy.start()
        sends.append(copy)
        return copy

    w_copies = []
    for i, w_hbm in enumerate((wq_hbm, wk_hbm, wv_hbm, wout_hbm)):
        w_copies.append(pltpu.make_async_copy(w_hbm, w_s.at[i], w_sem.at[i]))
    edge_copies = []
    for s in range(slots):
        edge_copies.append(pltpu.make_async_copy(edges_hbm.at[s], edge_s.at[s], edge_sem.at[s]))
        edge_copies[s].start()
    for copy in w_copies:
        copy.start()

    others = [(row, lax.rem(col + k, N_COL)) for k in range(1, N_COL)]
    peers = [on_x(1), on_x(3), on_x(2), on_y(1), on_y(3), on_y(2)] + others
    barrier = pltpu.get_barrier_semaphore()
    for peer in peers:
        pl.semaphore_signal(barrier, inc=1, device_id=peer, device_id_type=MESH)

    lane = iota(meta_own.shape, 1)
    words = jnp.zeros(meta_own.shape, jnp.int32)
    own_words = []
    for s in range(slots):
        tile = tile_ref[s]
        to, at = tile // SRC_BLOCKS, tile % SRC_BLOCKS
        t, o = at // PER_DEV, at % PER_DEV
        bx, by = t // NY, t % NY
        owner, p = to // PER_DEV, to % PER_DEV
        fields = [bx, by * PER_DEV + o, by, bx * PER_DEV + o, owner // 2, owner % 2 * PIECES + 2 * p, to]
        own_words.append(fields)
        for f, value in enumerate(fields):
            words = jnp.where(lane == f * slots + s, value, words)
    meta_own[...] = words
    for side in range(2):
        nodes_h[side] = nodes_ref[:, :, side * half : (side + 1) * half]

    def word(who, f, s):
        return own_words[s][f] if who is None else meta[who, 0, f * slots + s]

    pl.semaphore_wait(barrier, len(peers))

    sib_shard = push(
        nodes_h.at[other], pool_z.at[pl.ds(core * PIECES, PIECES)], pair_send_sem.at[0], pair_recv_sem.at[0], sibling
    )
    for i, (peer, there) in enumerate(
        (
            (on_x(3), 0),
            (on_x(1), 1),
            (on_x(2), 2),
            (on_y(3), 3),
            (on_y(1), 4),
            (on_y(2), 5),
            (sibling, 6),
            ((row, flip * 2 + 1), 7 + core),
            ((row, mirror * 2), 7 + core),
        )
    ):
        push(meta_own, meta_vmem.at[there], meta_send_sem.at[i], meta_recv_sem.at[there], peer)

    rings = [(pool_y, y, on_y, 0), (pool_x, x, on_x, 1)]
    low, high = pl.ds(0, HALF), pl.ds(HALF, HALF)
    ring_copies = [{}, {}]
    for step in range(2):
        for r, (pool, pos, on, side) in enumerate(rings):
            for way in range(2):
                part = step if way == 0 else 1 - step
                ring_copies[r][way, step] = push(
                    nodes_h.at[side, (low, high)[part]],
                    pool.at[pl.ds(pos * PIECES + part * HALF, HALF)],
                    ring_send_sem.at[r, way, step],
                    ring_recv_sem.at[r, way, step],
                    on(1 + 2 * way),
                )
        if step == 0:
            pair_own = push(
                nodes_h.at[core],
                pool_z.at[pl.ds((2 + core) * PIECES, PIECES)],
                pair_send_sem.at[1],
                pair_recv_sem.at[1],
                near,
            )
    for pool, pos, on, side in rings:
        pool[pl.ds(pos * PIECES, PIECES)] = nodes_h[side]
    pool_z[pl.ds(core * PIECES, PIECES)] = nodes_h[core]
    sib_shard.wait_recv()
    pair_sib = push(
        pool_z.at[pl.ds(other * PIECES, PIECES)],
        pool_z.at[pl.ds((2 + other) * PIECES, PIECES)],
        pair_send_sem.at[2],
        pair_recv_sem.at[2],
        near,
    )

    build_maps(wb_ref, wg_ref, wo_ref, mix_map, out_map)

    for r, (pool, pos, on, side) in enumerate(rings):
        for way in range(2):
            owner = lax.rem(pos + 3 - 2 * way, 4)
            ring_copies[r][way, 0].wait_recv()
            here = pool.at[pl.ds(owner * PIECES + way * HALF, HALF)]
            ring_copies[r][way, 2] = push(
                here, here, ring_send_sem.at[r, way, 2], ring_recv_sem.at[r, way, 2], on(1 + 2 * way)
            )

    def terms(s):
        edge_copies[s].wait()
        edge_terms(s, edge_s, mix_map, bias_s, gate_s)

    for i in range(9):
        remote(meta_own, meta_vmem.at[i], meta_send_sem.at[i], meta_recv_sem.at[i], sibling).wait_recv()
    to_smem = pltpu.make_async_copy(meta_vmem, meta, local_sem)
    to_smem.start()
    terms(0)
    to_smem.wait()

    def load(pool, block):
        return pool[pl.ds(block * 2, 2)]

    def load_z(who, s):
        group = jnp.where(word(who, 4, s) == near_z, 2 * PIECES, 0)
        return pool_z[pl.ds(group + word(who, 5, s), 2)]

    pair_own.wait_recv()
    pair_sib.wait_recv()
    wishes = []
    for b in range(batches):
        for d in range(2):
            for k in range(2):
                wish_send[b, d, k] = load_z(7 + d, 2 * b + k)
        wishes.append(
            push(wish_send.at[b], wish_recv.at[b], wish_send_sem.at[b], wish_recv_sem.at[b], far_pair)
        )

    fills = [(pool_y, x, on_x, 0, (0, 1, 2)), (pool_x, y, on_y, 2, (3, 4, 5))]
    fill_copies = {}

    def send_fill(f, way, b, part, value):
        fill_send[f, way, b, part] = value
        fill_copies[f, way, b, part] = push(
            fill_send.at[f, way, b, part],
            fill_recv.at[f, way, b, part],
            fill_send_sem.at[f, way, b, part],
            fill_recv_sem.at[f, way, b, part],
            fills[f][2](1 + 2 * way),
        )

    def fill_start(f, b):
        pool, pos, on, at, (plus, minus, far) = fills[f]
        for part in range(2):
            for way in range(2):
                who = far if part == 0 else (plus, minus)[way]
                s = 2 * b + (way if part == 0 else 1 - way)
                send_fill(f, way, b, part, load(pool, word(who, at + 1, s)))

    def fill_end(f, b):
        pool, pos, on, at, (plus, minus, far) = fills[f]
        for way in range(2):
            who, s = (plus, minus)[way], 2 * b + way
            fill_copies[f, way, b, 0].wait_recv()
            mine = load(pool, word(who, at + 1, s))
            send_fill(
                f, way, b, 2, jnp.where(word(who, at, s) == pos, mine, fill_recv[f, way, b, 0])
            )

    def dest_batch(b):
        wishes[b].wait_recv()
        for k in range(2):
            s = 2 * b + k
            for who, d in ((6, other), (None, core)):
                at = word(who, 4, s)
                inside = jnp.where(at == z, 1, jnp.where(at == near_z, 1, 0))
                value = jnp.where(inside == 1, load_z(who, s), wish_recv[b, d, k])
                if who is None:
                    dest_s[core, s] = value
                else:
                    core_send[s] = value
        here = pl.ds(2 * b, 2)
        return push(
            core_send.at[here], dest_s.at[core, here], core_send_sem.at[b], core_recv_sem.at[b], sibling
        )

    def source_batch(b):
        for f, (pool, pos, on, at, who) in enumerate(fills):
            for way in range(2):
                for part in (1, 2):
                    fill_copies[f, way, b, part].wait_recv()
            for k in range(2):
                s = 2 * b + k
                p = word(None, at, s)
                mine = load(pool, word(None, at + 1, s))
                direct, passed = fill_recv[f, 1 - k, b, 1], fill_recv[f, k, b, 2]
                beside = p == lax.rem(pos + 1 + 2 * k, 4)
                src_s[f, s] = jnp.where(p == pos, mine, jnp.where(beside, direct, passed))

    for f in range(2):
        for way in range(2):
            for step in (1, 2):
                ring_copies[f][way, step].wait_recv()
        fill_start(f, 0)
    dest_copies = [dest_batch(0)]
    for f in range(2):
        fill_end(f, 0)
        fill_start(f, 1)
    terms(1)
    dest_copies.append(dest_batch(1))
    for copy in w_copies:
        copy.wait()
    dest_copies[0].wait_recv()
    project(dest_s, 0, w_s.at[0], q_s)

    lives = [s < count_ref[0] for s in range(slots)]
    sib_copies, first_copies = [], []

    def attend_batch(b):
        for s in (2 * b, 2 * b + 1):
            attend(
                s, lives[s], q_s, k_s, v_s, bias_s, gate_s, score_s, weight_s, expo_s, numer_s, denom_s
            )
            here = pl.ds(2 * s, 2)
            sib_copies.append(
                push(numer_s.at[other, here], sib_numer.at[here], sib_send_sem.at[s], sib_recv_sem.at[s], sibling)
            )
        here = pl.ds(4 * b, 4)
        first_copies.append(
            push(
                numer_s.at[core, here],
                pair_numer.at[core, here],
                first_send_sem.at[b, 0],
                first_recv_sem.at[b, 0],
                far_pair,
            )
        )

    def pass_sibling(b):
        for s in (2 * b, 2 * b + 1):
            sib_copies[s].wait_recv()
        here = pl.ds(4 * b, 4)
        first_copies.append(
            push(
                sib_numer.at[here],
                pair_numer.at[other, here],
                first_send_sem.at[b, 1],
                first_recv_sem.at[b, 1],
                far_pair,
            )
        )

    def emit(s):
        edge_output(s, lives[s], gain_edge_ref, out_map, edge_s, score_s, mixed_s)

    source_batch(0)
    project(src_s, 0, w_s.at[1], k_s)
    project(src_s, 0, w_s.at[2], v_s)
    for f in range(2):
        fill_end(f, 1)
    attend_batch(0)
    pass_sibling(0)
    dest_copies[1].wait_recv()
    project(dest_s, 1, w_s.at[0], q_s)
    terms(2)
    terms(3)
    source_batch(1)
    project(src_s, 1, w_s.at[1], k_s)
    project(src_s, 1, w_s.at[2], v_s)
    attend_batch(1)
    pass_sibling(1)

    mine = [word(None, 6, s) for s in range(slots)]
    ids = [mine, [word(6, 6, s) for s in range(slots)]]
    ids += [[word(7 + d, 6, s) for s in range(slots)] for d in range(2)]

    def find(of, a):
        index, found = jnp.int32(0), jnp.int32(0)
        for s in range(slots):
            index = jnp.where(of[s] == a, s, index)
            found = jnp.where(of[s] == a, 1, found)
        return index, found

    def denom_of(owner, o):
        index, found = find(mine, owner * PER_DEV + o)
        d = denom_s[index]
        return jnp.where(found > 0, d, jnp.zeros_like(d))

    den_copies = []
    for k in range(1, N_COL):
        for o in range(PER_DEV):
            den_send[k, o] = denom_of(lax.rem(col + k, N_COL), o)
        den_copies.append(
            push(den_send.at[k], den_recv.at[k], den_send_sem.at[k], den_recv_sem.at[k], others[k - 1])
        )

    emit(0)
    for copy in first_copies:
        copy.wait_recv()

    def block_sum(at_z, at_core, o):
        a = (at_z * 2 + at_core) * PER_DEV + o
        total = jnp.zeros((2, BLOCK // 2, half), F32)
        for i, of in enumerate(ids):
            index, found = find(of, a)
            here = pl.ds(2 * index, 2)
            part = (numer_s[core, here] if i == 0 else sib_numer[here] if i == 1 else pair_numer[i - 2, here])
            total += jnp.where(found > 0, part, jnp.zeros_like(part)).astype(F32)
        return total

    sum_copies = []
    for i, at_core in enumerate((other, core)):
        for o in range(PER_DEV):
            sum_send[i, 2 * o : 2 * o + 2] = block_sum(near_z, at_core, o).astype(BF16)
        sum_copies.append(
            push(sum_send.at[i], sum_recv.at[i], sum_send_sem.at[i], sum_recv_sem.at[i], near)
        )
    emit(1)
    emit(2)
    sum_copies[0].wait_recv()
    for o in range(PER_DEV):
        here = slice(2 * o, 2 * o + 2)
        last_send[here] = (block_sum(z, other, o) + sum_recv[0, here].astype(F32)).astype(BF16)
    last_copy = push(last_send, last_s.at[core], last_sem.at[0], last_sem.at[1], sibling)
    emit(3)
    for copy in den_copies:
        copy.wait_recv()
    heads = iota((2 * HEADS, width), 0) & 7
    lanes = iota((2 * HEADS, width), 1)
    expand = where01((lanes >= heads * head_dim) & (lanes < (heads + 1) * head_dim))
    scales = []
    for o in range(PER_DEV):
        d = denom_of(col, o)
        for k in range(1, N_COL):
            d += den_recv[k, o]
        inverse = jnp.where(d > 0.0, 1.0 / jnp.where(d > 0.0, d, 1.0), 0.0)
        upper = inverse.astype(BF16).astype(F32)
        scales.append(dot(jnp.concatenate([upper, inverse - upper], axis=0).astype(BF16), expand, TN))
    sum_copies[1].wait_recv()
    for o in range(PER_DEV):
        here = slice(2 * o, 2 * o + 2)
        last_s[core, here] = (block_sum(z, core, o) + sum_recv[1, here].astype(F32)).astype(BF16)
    last_copy.wait_recv()
    for o in range(PER_DEV):
        here = slice(2 * o, 2 * o + 2)
        numer = jnp.concatenate([last_s[side, here].reshape(BLOCK, half) for side in range(2)], axis=1)
        attended = (numer.astype(F32) * scales[o]).astype(BF16)
        base = nodes_ref[here].reshape(BLOCK, width).astype(F32)
        mixed = base + dot(attended, w_s[3])
        mean = jnp.mean(mixed * mixed, axis=1, keepdims=True)
        nodes_out[o * BLOCK : (o + 1) * BLOCK] = (
            mixed * lax.rsqrt(mean + 1e-05) * gain_node_ref[...][None]
        ).astype(BF16)
    for copy in sends:
        copy.wait_send()


def on_device(
    nodes,
    w_query,
    w_key,
    w_value,
    w_out,
    w_edge_gate,
    w_edge_bias,
    w_edge_out,
    gain_node,
    gain_edge,
    edges,
    tile_list,
    tile_count,
):
    rows, width = nodes.shape
    slots = edges.shape[2]
    batches = slots // 2
    piece = rows // PIECES
    half = width // 2
    vm = pl.BlockSpec(memory_space=pltpu.VMEM)
    sm = pl.BlockSpec(memory_space=pltpu.SMEM)
    hbm = pl.BlockSpec(memory_space=pl.ANY)
    dma = pltpu.SemaphoreType.DMA
    v = pltpu.VMEM
    nodes_out, edges_out = pl.pallas_call(
        layer_kernel,
        in_specs=[sm, sm, sm] + [vm] * 5 + [hbm] * 5,
        out_specs=[vm, vm],
        out_shape=[v((rows, width), BF16), v((slots, CH, BLOCK, BLOCK), BF16)],
        scratch_shapes=[
            v((2, PIECES, piece, half), BF16),
            v((NY * PIECES, piece, half), BF16),
            v((NX * PIECES, piece, half), BF16),
            v((4 * PIECES, piece, half), BF16),
            v((2, 2, batches, 3, 2, piece, half), BF16),
            v((2, 2, batches, 3, 2, piece, half), BF16),
            v((batches, 2, 2, 2, piece, half), BF16),
            v((batches, 2, 2, 2, piece, half), BF16),
            v((slots, 2, piece, half), BF16),
            v((8, 128), jnp.int32),
            v((9, 8, 128), jnp.int32),
            pltpu.SMEM((9, 8, 128), jnp.int32),
            dma((2, 2, 3)),
            dma((2, 2, 3)),
            dma((3,)),
            dma((3,)),
            dma((2, 2, batches, 3)),
            dma((2, 2, batches, 3)),
            dma((batches,)),
            dma((batches,)),
            dma((9,)),
            dma((9,)),
            dma((batches,)),
            dma((batches,)),
            dma,
            v((4, width, width), BF16),
            v((2, slots, 2, piece, half), BF16),
            v((2, slots, 2, piece, half), BF16),
            v((slots, BLOCK, width), BF16),
            v((slots, BLOCK, width), BF16),
            v((slots, BLOCK, width), BF16),
            v((2 * HEADS * GROUP, CH * GROUP), BF16),
            v((CH * GROUP, 2 * HEADS * GROUP), BF16),
            v((slots, HEADS, BLOCK, BLOCK), F32),
            v((slots, HEADS, BLOCK, BLOCK), F32),
            v((slots, HEADS, BLOCK, BLOCK), BF16),
            v((HEADS, BLOCK, BLOCK), BF16),
            v((BLOCK, HEADS * BLOCK), BF16),
            v((CH * GROUP, 2 * BLOCK), F32),
            v((2, 2 * slots, piece, half), BF16),
            v((slots, HEADS, BLOCK), F32),
            dma((slots,)),
            dma((4,)),
            v((2 * slots, piece, half), BF16),
            v((2, 2 * slots, piece, half), BF16),
            v((2, PIECES, piece, half), BF16),
            v((2, PIECES, piece, half), BF16),
            v((PIECES, piece, half), BF16),
            v((2, PIECES, piece, half), BF16),
            v((N_COL, PER_DEV, HEADS, BLOCK), F32),
            v((N_COL, PER_DEV, HEADS, BLOCK), F32),
            dma((slots,)),
            dma((slots,)),
            dma((batches, 2)),
            dma((batches, 2)),
            dma((2,)),
            dma((2,)),
            dma((2,)),
            dma((N_COL,)),
            dma((N_COL,)),
        ],
        compiler_params=pltpu.CompilerParams(
            collective_id=0, has_side_effects=True, vmem_limit_bytes=50 * 1024 * 1024
        ),
        name="layer",
    )(
        tile_list.reshape(-1),
        tile_count.reshape(1),
        gain_edge,
        nodes.reshape(PIECES, piece, width),
        w_edge_bias.T,
        w_edge_gate.T,
        w_edge_out,
        gain_node,
        w_query,
        w_key,
        w_value,
        w_out,
        edges.reshape(slots, CH, BLOCK, BLOCK),
    )

    return (nodes_out, edges_out.reshape(edges.shape))


def solution(mesh):
    return jax.shard_map(
        on_device,
        mesh=mesh,
        in_specs=(
            P(("row", "col"), None),
            *[P()] * 9,
            P("row", "col", None, None, None, None),
            P("row", "col", None),
            P("row", "col"),
        ),
        out_specs=(P(("row", "col"), None), P("row", "col", None, None, None, None)),
        check_vma=False,
    )
```

time: 70 us -> 63.7 us (0.910)
  Pallas kernels: 64.4 us -> 58.1 us
    pallas_call x1, Pallas kernels: 64.4 us -> 58.1 us  [on_device(): pl.pallas_call(layer_kernel, in_specs=[sm, sm, sm] + [vm] * 5 + [hbm] * 5...]
where the time goes in v5:
time: 63.7 us; the launch traced here: 63.6 us
  Pallas kernels  58.1 us (91%)
  local copies, waits for them, and re-layouts  4.21 us (7%)
  between operations  1.29 us (2%)
    pallas_call x1, Pallas kernels, on_device(): pl.pallas_call(layer_kernel, in_specs=[sm, sm, sm] + [vm] * 5 + [hbm] * 5...  58.1 us
    unnamed x2, local copies, waits for them, and re-layouts  4.21 us

profile of v5, /device:TPU:1, one launch (start us, length us, event | category | flops | bytes accessed | tf_op | source)
XLA Modules:
  0.0 63.6 jit_solution(9208286869898952933)
XLA Ops:
  1.3 58.1 %layer.1 = (bf16[384,768]{1,0:T(8,128)(2,1)S(1)}, bf16[4,64,128,128]{3,2,1,0:T(8,128)(2,1)S(1)}) custom-call(s32[4]{0:T(128)} %bitcast.13, s32[1]{0:T(128)} %bitcast.7.count_ref, f32[64]{0:T(128)} %gain_edge_ref.1, bf16[6,64,768]{2,1,0:T(8,128)(2,1)} %bitcast.10, bf16[8,64]{1,0:T(8,128)(2,1)} %bitcast.11, bf16[8,64]{1,0:T(8,128)(2,1)} %bitcast.12, ...), custom_call_target="tpu_custom_call" | custom-call | tf_op jit(solution)/shard_map/layer/pallas_call | solution.py:641
  59.3 0.8 %copy.17 = bf16[384,768]{1,0:T(8,128)(2,1)} copy(bf16[384,768]{1,0:T(8,128)(2,1)S(1)} %get-tuple-element.6) | data formatting | bytes 1179648
  60.2 3.4 %copy.18 = bf16[1,1,4,64,128,128]{5,4,3,2,1,0:T(8,128)(2,1)} copy(bf16[1,1,4,64,128,128]{5,4,3,2,1,0:T(8,128)(2,1)S(1)} %bitcast.8) | data formatting | bytes 16777216

commit v6 on v5

--- a/solution.py
+++ b/solution.py
@@ -100,12 +100,11 @@
     lax.fori_loop(0, BLOCK // (2 * GROUP), pair, 0)
 
 
-def project(x_s, batch, w_s, y_s):
+def project(x_s, slot, w_s, y_s):
     width = w_s.shape[0]
-    slots = slice(2 * batch, 2 * batch + 2)
-    x = jnp.concatenate([x_s[side, slots].reshape(2 * BLOCK, width // 2) for side in range(2)], axis=1)
+    x = jnp.concatenate([x_s[side, slot].reshape(BLOCK, width // 2) for side in range(2)], axis=1)
     for n in range(0, width, 256):
-        y_s[slots, :, n : n + 256] = dot(x, w_s[:, n : n + 256]).astype(BF16).reshape(2, BLOCK, 256)
+        y_s[slot, :, n : n + 256] = dot(x, w_s[:, n : n + 256]).astype(BF16)
 
 
 def attend(slot, live, q_s, k_s, v_s, bias_s, gate_s, score_s, weight_s, expo_s, numer_s, denom_s):
@@ -189,6 +188,8 @@
     pool_z,
     fill_send,
     fill_recv,
+    pass_send,
+    pass_recv,
     wish_send,
     wish_recv,
     core_send,
@@ -201,6 +202,8 @@
     pair_recv_sem,
     fill_send_sem,
     fill_recv_sem,
+    pass_send_sem,
+    pass_recv_sem,
     wish_send_sem,
     wish_recv_sem,
     meta_send_sem,
@@ -250,7 +253,6 @@
     head_dim = width // HEADS
     half = width // 2
     slots = edge_s.shape[0]
-    batches = slots // 2
     other = 1 - core
     flip, mirror = z + 1 - 2 * (z % 2), NZ - 1 - z
     near_z = flip * other + mirror * core
@@ -302,8 +304,32 @@
 
     pl.semaphore_wait(barrier, len(peers))
 
+    rings = [(pool_y, y, on_y, 0), (pool_x, x, on_x, 1)]
+    low, high = pl.ds(0, HALF), pl.ds(HALF, HALF)
+    ring_copies = [{}, {}]
+
+    def ring_start(step):
+        for r, (pool, pos, on, side) in enumerate(rings):
+            for way in range(2):
+                part = step if way == 0 else 1 - step
+                ring_copies[r][way, step] = push(
+                    nodes_h.at[side, (low, high)[part]],
+                    pool.at[pl.ds(pos * PIECES + part * HALF, HALF)],
+                    ring_send_sem.at[r, way, step],
+                    ring_recv_sem.at[r, way, step],
+                    on(1 + 2 * way),
+                )
+
+    ring_start(0)
     sib_shard = push(
         nodes_h.at[other], pool_z.at[pl.ds(core * PIECES, PIECES)], pair_send_sem.at[0], pair_recv_sem.at[0], sibling
+    )
+    pair_own = push(
+        nodes_h.at[core],
+        pool_z.at[pl.ds((2 + core) * PIECES, PIECES)],
+        pair_send_sem.at[1],
+        pair_recv_sem.at[1],
+        near,
     )
     for i, (peer, there) in enumerate(
         (
@@ -319,29 +345,7 @@
         )
     ):
         push(meta_own, meta_vmem.at[there], meta_send_sem.at[i], meta_recv_sem.at[there], peer)
-
-    rings = [(pool_y, y, on_y, 0), (pool_x, x, on_x, 1)]
-    low, high = pl.ds(0, HALF), pl.ds(HALF, HALF)
-    ring_copies = [{}, {}]
-    for step in range(2):
-        for r, (pool, pos, on, side) in enumerate(rings):
-            for way in range(2):
-                part = step if way == 0 else 1 - step
-                ring_copies[r][way, step] = push(
-                    nodes_h.at[side, (low, high)[part]],
-                    pool.at[pl.ds(pos * PIECES + part * HALF, HALF)],
-                    ring_send_sem.at[r, way, step],
-                    ring_recv_sem.at[r, way, step],
-                    on(1 + 2 * way),
-                )
-        if step == 0:
-            pair_own = push(
-                nodes_h.at[core],
-                pool_z.at[pl.ds((2 + core) * PIECES, PIECES)],
-                pair_send_sem.at[1],
-                pair_recv_sem.at[1],
-                near,
-            )
+    ring_start(1)
     for pool, pos, on, side in rings:
         pool[pl.ds(pos * PIECES, PIECES)] = nodes_h[side]
     pool_z[pl.ds(core * PIECES, PIECES)] = nodes_h[core]
@@ -354,7 +358,12 @@
         near,
     )
 
+    def terms(s):
+        edge_copies[s].wait()
+        edge_terms(s, edge_s, mix_map, bias_s, gate_s)
+
     build_maps(wb_ref, wg_ref, wo_ref, mix_map, out_map)
+    terms(0)
 
     for r, (pool, pos, on, side) in enumerate(rings):
         for way in range(2):
@@ -365,19 +374,12 @@
                 here, here, ring_send_sem.at[r, way, 2], ring_recv_sem.at[r, way, 2], on(1 + 2 * way)
             )
 
-    def terms(s):
-        edge_copies[s].wait()
-        edge_terms(s, edge_s, mix_map, bias_s, gate_s)
-
     for i in range(9):
         remote(meta_own, meta_vmem.at[i], meta_send_sem.at[i], meta_recv_sem.at[i], sibling).wait_recv()
     to_smem = pltpu.make_async_copy(meta_vmem, meta, local_sem)
     to_smem.start()
-    terms(0)
+    terms(1)
     to_smem.wait()
-
-    def load(pool, block):
-        return pool[pl.ds(block * 2, 2)]
 
     def load_z(who, s):
         group = jnp.where(word(who, 4, s) == near_z, 2 * PIECES, 0)
@@ -386,147 +388,145 @@
     pair_own.wait_recv()
     pair_sib.wait_recv()
     wishes = []
-    for b in range(batches):
+    for s in range(slots):
         for d in range(2):
+            wish_send[s, d] = load_z(7 + d, s)
+        wishes.append(
+            push(wish_send.at[s], wish_recv.at[s], wish_send_sem.at[s], wish_recv_sem.at[s], far_pair)
+        )
+    terms(2)
+    terms(3)
+
+    fills = [(pool_y, x, on_x, 0, (0, 1, 2)), (pool_x, y, on_y, 2, (3, 4, 5))]
+    fill_copies, pass_copies = {}, {}
+
+    def fill_start(j):
+        for f, (pool, pos, on, at, (plus, minus, far)) in enumerate(fills):
+            for way in range(2):
+                who = (plus, minus)[way]
+                if j > 0:
+                    fill_send[f, way, j, 0] = pool[word(who, at + 1, j - 1) * 2 + 1 - way]
+                if j < slots:
+                    fill_send[f, way, j, 1] = pool[word(far, at + 1, j) * 2 + way]
+                part = pl.ds(1, 1) if j == 0 else pl.ds(0, 1) if j == slots else pl.ds(0, 2)
+                fill_copies[f, way, j] = push(
+                    fill_send.at[f, way, j, part],
+                    fill_recv.at[f, way, j, part],
+                    fill_send_sem.at[f, way, j],
+                    fill_recv_sem.at[f, way, j],
+                    on(1 + 2 * way),
+                )
+
+    def fill_pass(s):
+        for f, (pool, pos, on, at, (plus, minus, far)) in enumerate(fills):
+            for way in range(2):
+                who = (plus, minus)[way]
+                fill_copies[f, way, s].wait_recv()
+                mine = pool[word(who, at + 1, s) * 2 + way]
+                pass_send[f, way, s] = jnp.where(word(who, at, s) == pos, mine, fill_recv[f, way, s, 1])
+                pass_copies[f, way, s] = push(
+                    pass_send.at[f, way, s],
+                    pass_recv.at[f, way, s],
+                    pass_send_sem.at[f, way, s],
+                    pass_recv_sem.at[f, way, s],
+                    on(1 + 2 * way),
+                )
+        if s + 2 <= slots:
+            fill_start(s + 2)
+
+    def dest_start(s):
+        wishes[s].wait_recv()
+        for who, d in ((6, other), (None, core)):
+            at = word(who, 4, s)
+            inside = jnp.where(at == z, 1, jnp.where(at == near_z, 1, 0))
+            value = jnp.where(inside == 1, load_z(who, s), wish_recv[s, d])
+            if who is None:
+                dest_s[core, s] = value
+            else:
+                core_send[s] = value
+        return push(
+            core_send.at[s], dest_s.at[core, s], core_send_sem.at[s], core_recv_sem.at[s], sibling
+        )
+
+    def source(s):
+        if s == slots - 1:
+            for f in range(2):
+                for way in range(2):
+                    fill_copies[f, way, slots].wait_recv()
+        for f, (pool, pos, on, at, who) in enumerate(fills):
+            p = word(None, at, s)
+            for way in range(2):
+                pass_copies[f, way, s].wait_recv()
             for k in range(2):
-                wish_send[b, d, k] = load_z(7 + d, 2 * b + k)
-        wishes.append(
-            push(wish_send.at[b], wish_recv.at[b], wish_send_sem.at[b], wish_recv_sem.at[b], far_pair)
-        )
-
-    fills = [(pool_y, x, on_x, 0, (0, 1, 2)), (pool_x, y, on_y, 2, (3, 4, 5))]
-    fill_copies = {}
-
-    def send_fill(f, way, b, part, value):
-        fill_send[f, way, b, part] = value
-        fill_copies[f, way, b, part] = push(
-            fill_send.at[f, way, b, part],
-            fill_recv.at[f, way, b, part],
-            fill_send_sem.at[f, way, b, part],
-            fill_recv_sem.at[f, way, b, part],
-            fills[f][2](1 + 2 * way),
-        )
-
-    def fill_start(f, b):
-        pool, pos, on, at, (plus, minus, far) = fills[f]
-        for part in range(2):
-            for way in range(2):
-                who = far if part == 0 else (plus, minus)[way]
-                s = 2 * b + (way if part == 0 else 1 - way)
-                send_fill(f, way, b, part, load(pool, word(who, at + 1, s)))
-
-    def fill_end(f, b):
-        pool, pos, on, at, (plus, minus, far) = fills[f]
-        for way in range(2):
-            who, s = (plus, minus)[way], 2 * b + way
-            fill_copies[f, way, b, 0].wait_recv()
-            mine = load(pool, word(who, at + 1, s))
-            send_fill(
-                f, way, b, 2, jnp.where(word(who, at, s) == pos, mine, fill_recv[f, way, b, 0])
+                mine = pool[word(None, at + 1, s) * 2 + k]
+                direct, passed = fill_recv[f, 1 - k, s + 1, 0], pass_recv[f, k, s]
+                beside = p == lax.rem(pos + 1 + 2 * k, 4)
+                src_s[f, s, k] = jnp.where(p == pos, mine, jnp.where(beside, direct, passed))
+
+    lives = [s < count_ref[0] for s in range(slots)]
+    sib_copies, first_copies, dest_copies = [], [], []
+
+    def tile(s):
+        dest_copies[s].wait_recv()
+        project(dest_s, s, w_s.at[0], q_s)
+        source(s)
+        project(src_s, s, w_s.at[1], k_s)
+        project(src_s, s, w_s.at[2], v_s)
+        attend(s, lives[s], q_s, k_s, v_s, bias_s, gate_s, score_s, weight_s, expo_s, numer_s, denom_s)
+        here = pl.ds(2 * s, 2)
+        sib_copies.append(
+            push(numer_s.at[other, here], sib_numer.at[here], sib_send_sem.at[s], sib_recv_sem.at[s], sibling)
+        )
+        first_copies.append(
+            push(
+                numer_s.at[core, here],
+                pair_numer.at[core, here],
+                first_send_sem.at[s, 0],
+                first_recv_sem.at[s, 0],
+                far_pair,
             )
-
-    def dest_batch(b):
-        wishes[b].wait_recv()
-        for k in range(2):
-            s = 2 * b + k
-            for who, d in ((6, other), (None, core)):
-                at = word(who, 4, s)
-                inside = jnp.where(at == z, 1, jnp.where(at == near_z, 1, 0))
-                value = jnp.where(inside == 1, load_z(who, s), wish_recv[b, d, k])
-                if who is None:
-                    dest_s[core, s] = value
-                else:
-                    core_send[s] = value
-        here = pl.ds(2 * b, 2)
-        return push(
-            core_send.at[here], dest_s.at[core, here], core_send_sem.at[b], core_recv_sem.at[b], sibling
-        )
-
-    def source_batch(b):
-        for f, (pool, pos, on, at, who) in enumerate(fills):
-            for way in range(2):
-                for part in (1, 2):
-                    fill_copies[f, way, b, part].wait_recv()
-            for k in range(2):
-                s = 2 * b + k
-                p = word(None, at, s)
-                mine = load(pool, word(None, at + 1, s))
-                direct, passed = fill_recv[f, 1 - k, b, 1], fill_recv[f, k, b, 2]
-                beside = p == lax.rem(pos + 1 + 2 * k, 4)
-                src_s[f, s] = jnp.where(p == pos, mine, jnp.where(beside, direct, passed))
+        )
+
+    def pass_sibling(s):
+        sib_copies[s].wait_recv()
+        here = pl.ds(2 * s, 2)
+        first_copies.append(
+            push(
+                sib_numer.at[here],
+                pair_numer.at[other, here],
+                first_send_sem.at[s, 1],
+                first_recv_sem.at[s, 1],
+                far_pair,
+            )
+        )
+
+    def emit(s):
+        edge_output(s, lives[s], gain_edge_ref, out_map, edge_s, score_s, mixed_s)
 
     for f in range(2):
         for way in range(2):
             for step in (1, 2):
                 ring_copies[f][way, step].wait_recv()
-        fill_start(f, 0)
-    dest_copies = [dest_batch(0)]
-    for f in range(2):
-        fill_end(f, 0)
-        fill_start(f, 1)
-    terms(1)
-    dest_copies.append(dest_batch(1))
+    fill_start(0)
+    fill_start(1)
     for copy in w_copies:
         copy.wait()
-    dest_copies[0].wait_recv()
-    project(dest_s, 0, w_s.at[0], q_s)
-
-    lives = [s < count_ref[0] for s in range(slots)]
-    sib_copies, first_copies = [], []
-
-    def attend_batch(b):
-        for s in (2 * b, 2 * b + 1):
-            attend(
-                s, lives[s], q_s, k_s, v_s, bias_s, gate_s, score_s, weight_s, expo_s, numer_s, denom_s
-            )
-            here = pl.ds(2 * s, 2)
-            sib_copies.append(
-                push(numer_s.at[other, here], sib_numer.at[here], sib_send_sem.at[s], sib_recv_sem.at[s], sibling)
-            )
-        here = pl.ds(4 * b, 4)
-        first_copies.append(
-            push(
-                numer_s.at[core, here],
-                pair_numer.at[core, here],
-                first_send_sem.at[b, 0],
-                first_recv_sem.at[b, 0],
-                far_pair,
-            )
-        )
-
-    def pass_sibling(b):
-        for s in (2 * b, 2 * b + 1):
-            sib_copies[s].wait_recv()
-        here = pl.ds(4 * b, 4)
-        first_copies.append(
-            push(
-                sib_numer.at[here],
-                pair_numer.at[other, here],
-                first_send_sem.at[b, 1],
-                first_recv_sem.at[b, 1],
-                far_pair,
-            )
-        )
-
-    def emit(s):
-        edge_output(s, lives[s], gain_edge_ref, out_map, edge_s, score_s, mixed_s)
-
-    source_batch(0)
-    project(src_s, 0, w_s.at[1], k_s)
-    project(src_s, 0, w_s.at[2], v_s)
-    for f in range(2):
-        fill_end(f, 1)
-    attend_batch(0)
+    dest_copies.append(dest_start(0))
+    fill_pass(0)
+    dest_copies.append(dest_start(1))
+    fill_pass(1)
+    tile(0)
+    dest_copies.append(dest_start(2))
+    fill_pass(2)
     pass_sibling(0)
-    dest_copies[1].wait_recv()
-    project(dest_s, 1, w_s.at[0], q_s)
-    terms(2)
-    terms(3)
-    source_batch(1)
-    project(src_s, 1, w_s.at[1], k_s)
-    project(src_s, 1, w_s.at[2], v_s)
-    attend_batch(1)
+    tile(1)
+    dest_copies.append(dest_start(3))
+    fill_pass(3)
     pass_sibling(1)
+    tile(2)
+    pass_sibling(2)
+    tile(3)
+    pass_sibling(3)
 
     mine = [word(None, 6, s) for s in range(slots)]
     ids = [mine, [word(6, 6, s) for s in range(slots)]]
@@ -630,7 +630,6 @@
 ):
     rows, width = nodes.shape
     slots = edges.shape[2]
-    batches = slots // 2
     piece = rows // PIECES
     half = width // 2
     vm = pl.BlockSpec(memory_space=pltpu.VMEM)
@@ -648,10 +647,12 @@
             v((NY * PIECES, piece, half), BF16),
             v((NX * PIECES, piece, half), BF16),
             v((4 * PIECES, piece, half), BF16),
-            v((2, 2, batches, 3, 2, piece, half), BF16),
-            v((2, 2, batches, 3, 2, piece, half), BF16),
-            v((batches, 2, 2, 2, piece, half), BF16),
-            v((batches, 2, 2, 2, piece, half), BF16),
+            v((2, 2, slots + 1, 2, piece, half), BF16),
+            v((2, 2, slots + 1, 2, piece, half), BF16),
+            v((2, 2, slots, piece, half), BF16),
+            v((2, 2, slots, piece, half), BF16),
+            v((slots, 2, 2, piece, half), BF16),
+            v((slots, 2, 2, piece, half), BF16),
             v((slots, 2, piece, half), BF16),
             v((8, 128), jnp.int32),
             v((9, 8, 128), jnp.int32),
@@ -660,14 +661,16 @@
             dma((2, 2, 3)),
             dma((3,)),
             dma((3,)),
-            dma((2, 2, batches, 3)),
-            dma((2, 2, batches, 3)),
-            dma((batches,)),
-            dma((batches,)),
+            dma((2, 2, slots + 1)),
+            dma((2, 2, slots + 1)),
+            dma((2, 2, slots)),
+            dma((2, 2, slots)),
+            dma((slots,)),
+            dma((slots,)),
             dma((9,)),
             dma((9,)),
-            dma((batches,)),
-            dma((batches,)),
+            dma((slots,)),
+            dma((slots,)),
             dma,
             v((4, width, width), BF16),
             v((2, slots, 2, piece, half), BF16),
@@ -697,8 +700,8 @@
             v((N_COL, PER_DEV, HEADS, BLOCK), F32),
             dma((slots,)),
             dma((slots,)),
-            dma((batches, 2)),
-            dma((batches, 2)),
+            dma((slots, 2)),
+            dma((slots, 2)),
             dma((2,)),
             dma((2,)),
             dma((2,)),

time: 63.7 us -> 60 us (0.942)
  Pallas kernels: 58.1 us -> 54.1 us
    pallas_call x1, Pallas kernels: 58.1 us -> 54.1 us  [on_device(): pl.pallas_call(layer_kernel, in_specs=[sm, sm, sm] + [vm] * 5 + [hbm] * 5...]
where the time goes in v6:
time: 60 us; the launch traced here: 59.6 us
  Pallas kernels  54.1 us (90%)
  local copies, waits for them, and re-layouts  4.21 us (7%)
  between operations  1.29 us (2%)
    pallas_call x1, Pallas kernels, on_device(): pl.pallas_call(layer_kernel, in_specs=[sm, sm, sm] + [vm] * 5 + [hbm] * 5...  54.1 us
    unnamed x2, local copies, waits for them, and re-layouts  4.21 us

profile of v6, /device:TPU:1, one launch (start us, length us, event | category | flops | bytes accessed | tf_op | source)
XLA Modules:
  0.0 59.6 jit_solution(15731641652546614600)
XLA Ops:
  1.3 54.1 %layer.1 = (bf16[384,768]{1,0:T(8,128)(2,1)S(1)}, bf16[4,64,128,128]{3,2,1,0:T(8,128)(2,1)S(1)}) custom-call(s32[4]{0:T(128)} %bitcast.13, s32[1]{0:T(128)} %bitcast.7.count_ref, f32[64]{0:T(128)} %gain_edge_ref.1, bf16[6,64,768]{2,1,0:T(8,128)(2,1)} %bitcast.10, bf16[8,64]{1,0:T(8,128)(2,1)} %bitcast.11, bf16[8,64]{1,0:T(8,128)(2,1)} %bitcast.12, ...), custom_call_target="tpu_custom_call" | custom-call | tf_op jit(solution)/shard_map/layer/pallas_call | solution.py:640
  55.4 0.8 %copy.17 = bf16[384,768]{1,0:T(8,128)(2,1)} copy(bf16[384,768]{1,0:T(8,128)(2,1)S(1)} %get-tuple-element.6) | data formatting | bytes 1179648
  56.2 3.4 %copy.18 = bf16[1,1,4,64,128,128]{5,4,3,2,1,0:T(8,128)(2,1)} copy(bf16[1,1,4,64,128,128]{5,4,3,2,1,0:T(8,128)(2,1)S(1)} %bitcast.8) | data formatting | bytes 16777216

commit v7 on v6

--- a/solution.py
+++ b/solution.py
@@ -170,11 +170,11 @@
     tile_ref,
     count_ref,
     gain_edge_ref,
-    nodes_ref,
-    wb_ref,
-    wg_ref,
-    wo_ref,
-    gain_node_ref,
+    nodes_hbm,
+    wb_hbm,
+    wg_hbm,
+    wo_hbm,
+    gain_node_hbm,
     wq_hbm,
     wk_hbm,
     wv_hbm,
@@ -183,6 +183,12 @@
     nodes_out,
     edge_s,
     nodes_h,
+    wb_ref,
+    wg_ref,
+    wo_ref,
+    gain_node_ref,
+    total_s,
+    early_sem,
     pool_y,
     pool_x,
     pool_z,
@@ -266,6 +272,26 @@
         sends.append(copy)
         return copy
 
+    early = []
+    for side in range(2):
+        early.append(
+            pltpu.make_async_copy(
+                nodes_hbm.at[:, :, side * half : (side + 1) * half], nodes_h.at[side], early_sem.at[side]
+            )
+        )
+    for i, (a, b) in enumerate(
+        ((wb_hbm, wb_ref), (wg_hbm, wg_ref), (wo_hbm, wo_ref), (gain_node_hbm, gain_node_ref))
+    ):
+        early.append(pltpu.make_async_copy(a, b, early_sem.at[2 + i]))
+    for copy in early:
+        copy.start()
+
+    others = [(row, lax.rem(col + k, N_COL)) for k in range(1, N_COL)]
+    peers = [on_x(1), on_x(3), on_x(2), on_y(1), on_y(3), on_y(2)] + others
+    barrier = pltpu.get_barrier_semaphore()
+    for peer in peers:
+        pl.semaphore_signal(barrier, inc=1, device_id=peer, device_id_type=MESH)
+
     w_copies = []
     for i, w_hbm in enumerate((wq_hbm, wk_hbm, wv_hbm, wout_hbm)):
         w_copies.append(pltpu.make_async_copy(w_hbm, w_s.at[i], w_sem.at[i]))
@@ -275,12 +301,6 @@
         edge_copies[s].start()
     for copy in w_copies:
         copy.start()
-
-    others = [(row, lax.rem(col + k, N_COL)) for k in range(1, N_COL)]
-    peers = [on_x(1), on_x(3), on_x(2), on_y(1), on_y(3), on_y(2)] + others
-    barrier = pltpu.get_barrier_semaphore()
-    for peer in peers:
-        pl.semaphore_signal(barrier, inc=1, device_id=peer, device_id_type=MESH)
 
     lane = iota(meta_own.shape, 1)
     words = jnp.zeros(meta_own.shape, jnp.int32)
@@ -296,8 +316,8 @@
         for f, value in enumerate(fields):
             words = jnp.where(lane == f * slots + s, value, words)
     meta_own[...] = words
-    for side in range(2):
-        nodes_h[side] = nodes_ref[:, :, side * half : (side + 1) * half]
+    for copy in early[:2]:
+        copy.wait()
 
     def word(who, f, s):
         return own_words[s][f] if who is None else meta[who, 0, f * slots + s]
@@ -362,6 +382,8 @@
         edge_copies[s].wait()
         edge_terms(s, edge_s, mix_map, bias_s, gate_s)
 
+    for copy in early[2:]:
+        copy.wait()
     build_maps(wb_ref, wg_ref, wo_ref, mix_map, out_map)
     terms(0)
 
@@ -573,12 +595,15 @@
         sum_copies.append(
             push(sum_send.at[i], sum_recv.at[i], sum_send_sem.at[i], sum_recv_sem.at[i], near)
         )
+    for i, at_core in enumerate((other, core)):
+        for o in range(PER_DEV):
+            total_s[i, 2 * o : 2 * o + 2] = block_sum(z, at_core, o)
     emit(1)
     emit(2)
     sum_copies[0].wait_recv()
     for o in range(PER_DEV):
         here = slice(2 * o, 2 * o + 2)
-        last_send[here] = (block_sum(z, other, o) + sum_recv[0, here].astype(F32)).astype(BF16)
+        last_send[here] = (total_s[0, here] + sum_recv[0, here].astype(F32)).astype(BF16)
     last_copy = push(last_send, last_s.at[core], last_sem.at[0], last_sem.at[1], sibling)
     emit(3)
     for copy in den_copies:
@@ -597,20 +622,51 @@
     sum_copies[1].wait_recv()
     for o in range(PER_DEV):
         here = slice(2 * o, 2 * o + 2)
-        last_s[core, here] = (block_sum(z, core, o) + sum_recv[1, here].astype(F32)).astype(BF16)
+        last_s[core, here] = (total_s[1, here] + sum_recv[1, here].astype(F32)).astype(BF16)
     last_copy.wait_recv()
     for o in range(PER_DEV):
         here = slice(2 * o, 2 * o + 2)
         numer = jnp.concatenate([last_s[side, here].reshape(BLOCK, half) for side in range(2)], axis=1)
         attended = (numer.astype(F32) * scales[o]).astype(BF16)
-        base = nodes_ref[here].reshape(BLOCK, width).astype(F32)
-        mixed = base + dot(attended, w_s[3])
+        base = jnp.concatenate([nodes_h[side, here].reshape(BLOCK, half) for side in range(2)], axis=1)
+        mixed = base.astype(F32) + dot(attended, w_s[3])
         mean = jnp.mean(mixed * mixed, axis=1, keepdims=True)
         nodes_out[o * BLOCK : (o + 1) * BLOCK] = (
             mixed * lax.rsqrt(mean + 1e-05) * gain_node_ref[...][None]
         ).astype(BF16)
     for copy in sends:
         copy.wait_send()
+
+
+def store_kernel(nodes_ref, edge_ref, nodes_out, edges_out, sem):
+    slots = edge_ref.shape[0]
+    copies = [pltpu.make_async_copy(nodes_ref, nodes_out, sem.at[slots])]
+    for s in range(slots):
+        copies.append(pltpu.make_async_copy(edge_ref.at[s], edges_out.at[s], sem.at[s]))
+    for copy in copies:
+        copy.start()
+    for copy in copies:
+        copy.wait()
+
+
+def store_call(nodes_new, edges_new):
+    vm = pl.BlockSpec(memory_space=pltpu.VMEM)
+    hbm = pl.BlockSpec(memory_space=pl.ANY)
+    return pl.pallas_call(
+        store_kernel,
+        in_specs=[vm, vm],
+        out_specs=[hbm, hbm],
+        out_shape=[
+            jax.ShapeDtypeStruct(nodes_new.shape, BF16),
+            jax.ShapeDtypeStruct(edges_new.shape, BF16),
+        ],
+        scratch_shapes=[pltpu.SemaphoreType.DMA((edges_new.shape[0] + 1,))],
+        compiler_params=pltpu.CompilerParams(vmem_limit_bytes=1 * 1024 * 1024),
+        name="store",
+    )(
+        pltpu.with_memory_space_constraint(nodes_new, pltpu.VMEM),
+        pltpu.with_memory_space_constraint(edges_new, pltpu.VMEM),
+    )
 
 
 def on_device(
@@ -639,11 +695,17 @@
     v = pltpu.VMEM
     nodes_out, edges_out = pl.pallas_call(
         layer_kernel,
-        in_specs=[sm, sm, sm] + [vm] * 5 + [hbm] * 5,
+        in_specs=[sm, sm, sm] + [hbm] * 10,
         out_specs=[vm, vm],
         out_shape=[v((rows, width), BF16), v((slots, CH, BLOCK, BLOCK), BF16)],
         scratch_shapes=[
             v((2, PIECES, piece, half), BF16),
+            v((HEADS, CH), BF16),
+            v((HEADS, CH), BF16),
+            v((HEADS, CH), F32),
+            v((width,), F32),
+            v((2, PIECES, piece, half), F32),
+            dma((6,)),
             v((NY * PIECES, piece, half), BF16),
             v((NX * PIECES, piece, half), BF16),
             v((4 * PIECES, piece, half), BF16),
@@ -709,7 +771,7 @@
             dma((N_COL,)),
         ],
         compiler_params=pltpu.CompilerParams(
-            collective_id=0, has_side_effects=True, vmem_limit_bytes=50 * 1024 * 1024
+            collective_id=0, has_side_effects=True, vmem_limit_bytes=48 * 1024 * 1024
         ),
         name="layer",
     )(
@@ -728,6 +790,7 @@
         edges.reshape(slots, CH, BLOCK, BLOCK),
     )
 
+    nodes_out, edges_out = store_call(nodes_out, edges_out)
     return (nodes_out, edges_out.reshape(edges.shape))
 
 

time: 60 us -> 58.9 us (0.982)
  local copies, waits for them, and re-layouts: 4.21 us -> 0 us
  Pallas kernels: 54.1 us -> 57.2 us
    unnamed x2 -> x0, local copies, waits for them, and re-layouts: 4.21 us -> none
    pallas_call x1 -> x2, Pallas kernels: 54.1 us -> 57.2 us  [the longest x1 53.6 us: on_device(): pl.pallas_call(layer_kernel, in_specs=[sm, sm, sm] + [hbm] * 10, out_spec...]
where the time goes in v7:
time: 58.9 us; the launch traced here: 58.5 us
  Pallas kernels  57.2 us (97%)
  between operations  1.29 us (2%)
    pallas_call x1, Pallas kernels, on_device(): pl.pallas_call(layer_kernel, in_specs=[sm, sm, sm] + [hbm] * 10, out_spec...  53.6 us
    pallas_call x1, Pallas kernels, store_call(): pl.pallas_call(store_kernel, in_specs=[vm, vm], out_specs=[hbm, hbm], out...  3.57 us

profile of v7, /device:TPU:1, one launch (start us, length us, event | category | flops | bytes accessed | tf_op | source)
XLA Modules:
  0.0 58.5 jit_solution(7688388232426723606)
XLA Ops:
  1.3 53.6 %layer.1 = (bf16[384,768]{1,0:T(8,128)(2,1)S(1)}, bf16[4,64,128,128]{3,2,1,0:T(8,128)(2,1)S(1)}) custom-call(s32[4]{0:T(128)} %bitcast.12, s32[1]{0:T(128)} %bitcast.7.count_ref, f32[64]{0:T(128)} %gain_edge_ref.1, bf16[6,64,768]{2,1,0:T(8,128)(2,1)} %bitcast.9, bf16[8,64]{1,0:T(8,128)(2,1)} %bitcast.10, bf16[8,64]{1,0:T(8,128)(2,1)} %bitcast.11, ...), custom_call_target="tpu_custom_call" | custom-call | tf_op jit(solution)/shard_map/layer/pallas_call | solution.py:696
  54.9 3.6 %store.1 = (bf16[384,768]{1,0:T(8,128)(2,1)}, bf16[4,64,128,128]{3,2,1,0:T(8,128)(2,1)}) custom-call(bf16[384,768]{1,0:T(8,128)(2,1)S(1)} %get-tuple-element.6.nodes_ref, bf16[4,64,128,128]{3,2,1,0:T(8,128)(2,1)S(1)} %get-tuple-element.7.edge_ref), custom_call_target="tpu_custom_call" | custom-call | tf_op jit(solution)/shard_map/store/pallas_call | solution.py:655

commit v8 on v7

--- a/solution.py
+++ b/solution.py
@@ -417,7 +417,6 @@
             push(wish_send.at[s], wish_recv.at[s], wish_send_sem.at[s], wish_recv_sem.at[s], far_pair)
         )
     terms(2)
-    terms(3)
 
     fills = [(pool_y, x, on_x, 0, (0, 1, 2)), (pool_x, y, on_y, 2, (3, 4, 5))]
     fill_copies, pass_copies = {}, {}
@@ -531,6 +530,7 @@
                 ring_copies[f][way, step].wait_recv()
     fill_start(0)
     fill_start(1)
+    terms(3)
     for copy in w_copies:
         copy.wait()
     dest_copies.append(dest_start(0))

time: 58.9 us -> 58.4 us (level)
  no operation moved by 1% of the time
where the time goes in v8:
time: 58.4 us; the launch traced here: 58.3 us
  Pallas kernels  57 us (98%)
  between operations  1.29 us (2%)
    pallas_call x1, Pallas kernels, on_device(): pl.pallas_call(layer_kernel, in_specs=[sm, sm, sm] + [hbm] * 10, out_spec...  53.4 us
    pallas_call x1, Pallas kernels, store_call(): pl.pallas_call(store_kernel, in_specs=[vm, vm], out_specs=[hbm, hbm], out...  3.57 us

profile of v8, /device:TPU:1, one launch (start us, length us, event | category | flops | bytes accessed | tf_op | source)
XLA Modules:
  0.0 58.3 jit_solution(6872741533549499470)
XLA Ops:
  1.3 53.4 %layer.1 = (bf16[384,768]{1,0:T(8,128)(2,1)S(1)}, bf16[4,64,128,128]{3,2,1,0:T(8,128)(2,1)S(1)}) custom-call(s32[4]{0:T(128)} %bitcast.12, s32[1]{0:T(128)} %bitcast.7.count_ref, f32[64]{0:T(128)} %gain_edge_ref.1, bf16[6,64,768]{2,1,0:T(8,128)(2,1)} %bitcast.9, bf16[8,64]{1,0:T(8,128)(2,1)} %bitcast.10, bf16[8,64]{1,0:T(8,128)(2,1)} %bitcast.11, ...), custom_call_target="tpu_custom_call" | custom-call | tf_op jit(solution)/shard_map/layer/pallas_call | solution.py:696
  54.7 3.6 %store.1 = (bf16[384,768]{1,0:T(8,128)(2,1)}, bf16[4,64,128,128]{3,2,1,0:T(8,128)(2,1)}) custom-call(bf16[384,768]{1,0:T(8,128)(2,1)S(1)} %get-tuple-element.6.nodes_ref, bf16[4,64,128,128]{3,2,1,0:T(8,128)(2,1)S(1)} %get-tuple-element.7.edge_ref), custom_call_target="tpu_custom_call" | custom-call | tf_op jit(solution)/shard_map/store/pallas_call | solution.py:655
